TPU v7x, 512 devices: a whole 4x4x16 slice. The times are simulated.
512 devices in a mesh: row: 32 (over y, x, core), col: 16 (over z).
Axes of the slice: x: 4, y: 4, z: 16, core: 2. Of those that a mesh axis runs over, the one named last changes fastest.
Arguments:
- columns_x: bfloat16 [32, 262144], P(None, ('row', 'col')), may hold values from -6 to 6
- col_basis: bfloat16 [1024, 64, 256], P(('row', 'col')), may hold values from -0.375 to 0.375
- col_links: bfloat16 [1024, 4096], P(('row', 'col')), may hold values from -0.5 to 0.5
- col_top_links: bfloat16 [16, 48, 4096], P('col'), may hold values from -0.5 to 0.5
- row_basis: bfloat16 [1024, 64, 256], P(('row', 'col')), may hold values from -0.75 to 0.75
- row_links: bfloat16 [32, 56, 4096], P('row'), may hold values from -0.5 to 0.5
- coupling: bfloat16 [65536, 4096], P(('row', 'col')), may hold values from -0.09375 to 0.09375
- coupling_rows: int32 [2048, 32], P(('row', 'col')), may hold values from 0 to 31, as said below
- coupling_cols: int32 [2048, 32], P(('row', 'col')), may hold values from 0 to 63, as said below
- near_blocks: bfloat16 [4096, 256, 256], P(('row', 'col')), may hold values from -0.1875 to 0.1875
- near_rows: int32 [4096], P(('row', 'col')), may hold values from 0 to 1
- near_cols: int32 [4096], P(('row', 'col')), may hold values from 0 to 1
Outputs:
- products: bfloat16 [32, 262144], P(None, ('row', 'col'))
Inputs may be any that keep to these rules, and one draw needn't show every extreme that they name: `coupling_rows`: in list row j the level is l = j mod 4, and the entry names a row cluster of level l of the row tree of the device's row index, below 32 / 2**l. `coupling_cols`: in list row j the level is l = j mod 4, and the entry names a column cluster of level l of the column tree of the device's col index, below 64 / 2**l. `near_rows`: a row leaf of the device's own part, numbered within it. `near_cols`: a column leaf of the device's own part, numbered within it.
All inputs are finite; a program needn't handle non-finite values.
Results may differ from a plain program's by a relative error of at most 0.02.
Values may be sent and summed in bfloat16 or wider, within the bound.
No kernel may reach another device: no remote copies, remote signals or barrier semaphores. Data moves between devices by JAX's collectives and lax.ppermute only.
A program may use at most 64 MiB of HBM per device.

v0:
```python
import jax
import jax.numpy as jnp
from jax import lax
from jax.sharding import PartitionSpec as P

HIGHEST = lax.Precision.HIGHEST


def as_sent(shard):
    return jax.tree.map(lambda a: a.astype(jnp.bfloat16) if a.dtype == jnp.float32 else a, shard)


def pair_reduce(children, links):
    terms = jnp.einsum("pnk,pkj->pnj", children, links, preferred_element_type=jnp.float32)
    return terms.reshape(terms.shape[0] // 2, 2, terms.shape[1], terms.shape[2]).sum(axis=1)


def descend(parents, links, vectors, width):
    doubled = jnp.repeat(parents.reshape(-1, vectors, width), 2, axis=0)
    matrices = links.astype(jnp.float32).reshape(links.shape[0], width, width)
    pushed = jnp.einsum("pnk,pkj->pnj", doubled, matrices, precision=HIGHEST)
    return pushed.reshape(pushed.shape[0], vectors * width)


def share_level(moments, packed):
    return lax.all_gather(moments.reshape(moments.shape[0], packed), "row", axis=0, tiled=True)


def local(
    columns_x,
    col_basis,
    col_links,
    col_top_links,
    row_basis,
    row_links,
    coupling,
    coupling_rows,
    coupling_cols,
    near_blocks,
    near_rows,
    near_cols,
):
    leaves, width, leaf_size = col_basis.shape
    vectors = columns_x.shape[0]
    levels_dev = leaves.bit_length()
    levels_all = coupling_rows.shape[0]
    blocks = coupling_rows.shape[1]
    cols_axis = lax.axis_size("col")
    row_leaves = cols_axis * leaves
    packed = vectors * width
    local_x = columns_x.reshape(vectors, leaves, leaf_size).transpose(1, 0, 2)
    moments = jnp.einsum(
        "inl,ikl->ink", local_x, col_basis, preferred_element_type=jnp.float32
    ).astype(jnp.bfloat16)
    own_levels = [moments]
    gathered = []
    gathered.append(share_level(moments, packed))
    offset = 0
    depth = 1
    count = leaves >> depth - 1
    links = col_links.reshape(count, width, width)
    moments = pair_reduce(moments, links).astype(jnp.bfloat16)
    offset += count
    own_levels.append(moments)
    gathered.append(share_level(moments, packed))
    col_tree = [item.reshape(item.shape[0], vectors, width) for item in gathered]
    current = col_tree[-1]
    top_links = col_top_links[0]
    offset = 0
    for depth in range(levels_dev, levels_all):
        count = current.shape[0]
        current = pair_reduce(
            current, top_links[offset : offset + count].reshape(count, width, width)
        ).astype(jnp.bfloat16)
        offset += count
        col_tree.append(current)
    partials = []
    for depth in range(levels_all):
        count = row_leaves >> depth
        picked = jnp.take(col_tree[depth], coupling_cols[depth], axis=0)
        matrices = coupling[depth * blocks : (depth + 1) * blocks].reshape(blocks, width, width)
        terms = jnp.einsum("bnk,bkj->bnj", picked, matrices, preferred_element_type=jnp.float32)
        owners = (
            coupling_rows[depth][None, :] == jnp.arange(count, dtype=jnp.int32)[:, None]
        ).astype(jnp.float32)
        partials.append(jnp.dot(owners, terms.reshape(blocks, packed), precision=HIGHEST))
    tree_links = row_links[0]
    upper = jax.tree.map(
        lambda part: part.astype(jnp.float32),
        lax.psum(as_sent(tuple(partials[levels_dev:])), "col"),
    )
    running = upper[-1]
    for depth in range(levels_all - 2, levels_dev - 2, -1):
        count = row_leaves >> depth
        start = 2 * (row_leaves - count)
        pushed = descend(running, tree_links[start : start + count], vectors, width)
        running = upper[depth - levels_dev] + pushed if depth >= levels_dev else pushed
    device_col = lax.axis_index("col")
    running = lax.dynamic_slice_in_dim(running, device_col, 1, 0)
    totals = []
    for depth in range(levels_dev):
        totals.append(
            lax.psum_scatter(
                partials[depth].astype(jnp.bfloat16), "col", scatter_dimension=0, tiled=True
            ).astype(jnp.float32)
        )
    running = totals[levels_dev - 1] + running
    depth = 0
    count = row_leaves >> depth
    start = 2 * (row_leaves - count) + device_col * (leaves >> depth)
    own_links = lax.dynamic_slice_in_dim(tree_links, start, leaves >> depth, 0)
    running = totals[depth] + descend(running, own_links, vectors, width)
    leaf_local = running.astype(jnp.bfloat16).reshape(leaves, vectors, width)
    distant = jnp.einsum("ink,ikl->inl", leaf_local, row_basis, preferred_element_type=jnp.float32)
    chosen = jnp.take(local_x, near_cols, axis=0)
    nearby = jnp.einsum("bnl,blm->bnm", chosen, near_blocks, preferred_element_type=jnp.float32)
    targets = (near_rows[None, :] == jnp.arange(leaves, dtype=jnp.int32)[:, None]).astype(
        jnp.float32
    )
    summed = jnp.dot(
        targets, nearby.reshape(nearby.shape[0], vectors * leaf_size), precision=HIGHEST
    )
    result = (distant + summed.reshape(leaves, vectors, leaf_size)).astype(jnp.bfloat16)
    return result.transpose(1, 0, 2).reshape(vectors, leaves * leaf_size)


def solution(mesh):
    in_specs = (
        P(None, ("row", "col")),
        P(("row", "col"), None, None),
        P(("row", "col"), None),
        P("col", None, None),
        P(("row", "col"), None, None),
        P("row", None, None),
        P(("row", "col"), None),
        P(("row", "col"), None),
        P(("row", "col"), None),
        P(("row", "col"), None, None),
        P(("row", "col")),
        P(("row", "col")),
    )
    out_specs = P(None, ("row", "col"))
    return jax.shard_map(local, mesh=mesh, in_specs=in_specs, out_specs=out_specs, check_vma=False)
```

profile of v0, /device:TPU:2, one launch (start us, length us, event | category | flops | bytes accessed | tf_op | source)
XLA Modules:
  0.0 213.6 jit_solution(9792079686458260465)
XLA Ops:
  6.5 0.9 fusion.36
  7.4 1.3 fusion.44
  8.7 0.5 reshape.279
  9.3 0.2 copy-done.5
  9.4 0.1 reshape.277
  9.6 0.6 copy-done.2
  10.2 0.1 convolution_convert_fusion.4
  10.3 0.1 reshape.346
  10.4 0.2 fusion.2
  10.7 27.6 %all-gather.1 = bf16[32,1,2048]{2,1,0:T(2,128)(2,1)S(1)} all-gather(bf16[1,1,2048]{2,1,0:T(2,128)(2,1)S(1)} %reshape.348), channel_id=1, replica_groups=mesh['row'=32,'col'=16] {'row'}, dimensions={0}, use_global_device_ids=true | all-gather | bytes 135168 | tf_op jit(solution)/shard_map/all_gather | solution.py:26
  38.3 0.7 reduce.2
  39.0 0.2 reshape.278
  39.3 0.6 gather_fusion.1
  39.9 0.3 fusion.7
  40.2 0.2 reshape.280
  40.4 0.5 copy-done.7
  40.9 0.5 reshape.275
  41.5 22.1 %all-gather = bf16[32,2,2048]{2,1,0:T(2,128)(2,1)S(1)} all-gather(bf16[1,2,2048]{2,1,0:T(2,128)(2,1)S(1)} %reshape.346), channel_id=1, replica_groups=mesh['row'=32,'col'=16] {'row'}, dimensions={0}, use_global_device_ids=true | all-gather | bytes 270336 | tf_op jit(solution)/shard_map/all_gather | solution.py:26
  63.5 0.4 reshape.274
  63.9 0.6 gather_fusion
  64.5 0.3 fusion.9
  64.8 0.2 reshape.276
  65.0 0.8 convolution_convert_fusion.1
  65.9 0.9 convolution_convert_fusion
  66.8 0.7 copy-done.9
  67.6 0.3 copy-done.1
  67.9 0.1 reshape.300
  68.0 0.5 reshape.287
  68.5 0.4 slice-done
  68.9 0.5 reshape.281
  69.5 0.3 bitcast_reduce_fusion
  69.7 0.6 slice-done.1
  70.4 0.2 reshape.285
  70.6 0.2 bitcast_reduce_fusion.1
  70.8 0.6 gather_fusion.3
  71.4 0.3 fusion.3
  71.8 0.2 reshape.288
  72.0 0.2 convolution_convert_fusion.3
  72.2 0.1 reshape.289
  72.3 0.5 reshape.283
  72.8 0.6 gather_fusion.2
  73.4 0.3 fusion.5
  73.8 0.2 reshape.284
  73.9 0.6 slice-done.2
  74.6 0.2 reshape.292
  74.8 0.2 convolution_convert_fusion.2
  75.0 60.4 %all-reduce.2 = (bf16[4,32,64]{2,1,0:T(8,128)(2,1)S(1)}, bf16[8,2048]{1,0:T(8,128)(2,1)S(1)}) all-reduce(bf16[4,32,64]{2,1,0:T(8,128)(2,1)S(1)} %reshape.289, bf16[8,2048]{1,0:T(8,128)(2,1)S(1)} %convolution_convert_fusion.2), channel_id=1, replica_groups=mesh['row'=32,'col'=16] {'col'}, use_global_device_ids=true, to_apply=%region_5.6 | all-reduce | flops 24576 | bytes 98304 | tf_op jit(solution)/shard_map/psum | solution.py:90
  135.4 0.2 fusion.47
  135.6 0.1 reshape.293
  135.8 0.8 slice-done.3
  136.6 0.2 reshape.296
  136.9 0.3 fusion.48
  137.2 0.1 reshape.297
  137.3 1.3 dynamic-slice.1
  139.3 0.6 gather_fusion.4
  139.9 0.3 convolution_bitcast_fusion
  140.2 0.3 copy-done.8
  140.5 0.4 fusion.29
  140.9 62.5 %all-reduce.6.cloned.1.call-done = (bf16[16,2048]{1,0:T(8,128)(2,1)}, bf16[32,2048]{1,0:T(8,128)(2,1)}) async-done(((bf16[16,2048]{1,0:T(8,128)(2,1)}, bf16[32,2048]{1,0:T(8,128)(2,1)}), (bf16[16,2048]{1,0:T(8,128)(2,1)}, bf16[32,2048]{1,0:T(8,128)(2,1)})) %all-reduce.6.cloned.1.call-update) | async-done | bytes 196624
  203.4 1.4 fusion.25
  204.9 0.1 fusion.22
  205.1 0.8 add_convert_fusion
  206.0 0.1 fusion.1
  206.2 0.6 copy.23
  (38 shorter events, 0.7 us)
Async XLA Ops:
  6.5 133.3 %copy-start = (bf16[8,256,256]{2,1,0:T(8,128)(2,1)S(1)}, bf16[8,256,256]{2,1,0:T(8,128)(2,1)}, u32[]{:S(2)}) copy-start(bf16[8,256,256]{2,1,0:T(8,128)(2,1)} %param.21) | copy-start | bytes 3145732
  6.5 0.9 copy-start.6
  6.5 196.8 %all-reduce.6.cloned.1.call-start = ((), (), s32[]{:S(2)}) async-start(), calls=%async_computation | async-start | bytes 393216
  8.7 0.7 copy-start.5
  8.7 0.8 copy-start.3
  9.4 0.8 copy-start.2
  40.2 0.7 copy-start.7
  66.8 1.0 copy-start.1
  66.8 0.7 copy-start.9
  68.0 1.0 slice-start
  69.5 0.9 slice-start.1
  73.7 0.8 slice-start.2
  135.7 0.9 slice-start.3
  139.8 0.7 copy-start.8
  205.0 1.0 copy-start.4
Sparse Core Ops, SparseCore 0:
  66.9 136.4 all-reduce.5
where the time goes:
time: 214 us
  blocking collectives  110 us (51%)
  waiting for transfers between devices  62.5 us (29%)
  local copies, waits for them, and re-layouts  17 us (8%)
  between operations  14.4 us (7%)
  matrix products  5.74 us (3%)
  other arithmetic  3.87 us (2%)
    unnamed x2, waiting for transfers between devices  62.5 us
    psum x1, blocking collectives, local(): lax.psum(as_sent(tuple(partials[levels_dev:])), 'col')  60.4 us
    all_gather x2, blocking collectives, share_level(): lax.all_gather(moments.reshape(moments.shape[0], packed), 'row', axis=0,...  49.7 us
  transfers between devices with their start and end apart: 1, of which 1 were waited for; matrix products, arithmetic and copies ran while one was open for 4% of the time, Pallas kernels for 0%

commit v1 on v0

v1 whole, which is shorter than its diff:
```python
import jax
import jax.numpy as jnp
from jax import lax
from jax.experimental import pallas as pl
from jax.experimental.pallas import tpu as pltpu
from jax.sharding import PartitionSpec as P

F32 = jnp.float32
BF16 = jnp.bfloat16


def dot(a, b):
    return jnp.dot(a, b, preferred_element_type=F32)


def vmem():
    return pl.BlockSpec(memory_space=pltpu.VMEM)


def smem():
    return pl.BlockSpec(memory_space=pltpu.SMEM)


def moments_kernel(x_ref, basis_ref, links_ref, out_ref):
    leaves = []
    for i in range(2):
        moment = lax.dot_general(
            x_ref[:, 256 * i : 256 * (i + 1)],
            basis_ref[i],
            (((1,), (1,)), ((), ())),
            preferred_element_type=F32,
        )
        leaves.append(moment.astype(BF16))
    parent = dot(leaves[0], links_ref[0]) + dot(leaves[1], links_ref[1])
    low = jnp.concatenate(leaves, axis=1)
    high = jnp.concatenate([parent[:16], parent[16:]], axis=1).astype(BF16)
    for r in range(out_ref.shape[0]):
        out_ref[r, 0:32, :] = low
        out_ref[r, 32:48, :] = high


def tree_kernel(rows_ref, cols_ref, got_ref, top_ref, coupling_ref, links_ref, out_ref, mom, acc):
    for a in range(32):
        both = got_ref[a, 0:32, :]
        mom[2 * a] = both[:, 0:64]
        mom[2 * a + 1] = both[:, 64:128]
        parent = got_ref[a, 32:48, :]
        mom[64 + a, 0:16] = parent[:, 0:64]
        mom[64 + a, 16:32] = parent[:, 64:128]
    for p in range(16):
        total = dot(mom[64 + 2 * p], top_ref[2 * p]) + dot(mom[65 + 2 * p], top_ref[2 * p + 1])
        mom[96 + p] = total.astype(BF16)
    for p in range(8):
        total = dot(mom[96 + 2 * p], top_ref[32 + 2 * p]) + dot(mom[97 + 2 * p], top_ref[33 + 2 * p])
        mom[112 + p] = total.astype(BF16)
    acc[...] = jnp.zeros_like(acc)
    for depth in range(4):
        first_col = 128 - (128 >> depth)
        first_row = 64 - (64 >> depth)
        for s in range(32):
            q = first_col + cols_ref[depth, s]
            p = first_row + rows_ref[depth, s]
            acc[p] += dot(mom[q], coupling_ref[depth * 32 + s])
    for depth in (2, 1, 0):
        count = 32 >> depth
        first = 64 - (64 >> depth)
        start = 2 * (32 - count)
        for p in range(count):
            parent = acc[first + count + p // 2].astype(BF16)
            acc[first + p] += dot(parent, links_ref[start + p])
    for b in range(16):
        out_ref[b, :, 0:64] = acc[2 * b].astype(BF16)
        out_ref[b, :, 64:128] = acc[2 * b + 1].astype(BF16)


def output_kernel(rows_ref, cols_ref, got_ref, basis_ref, x_ref, near_ref, out_ref, acc):
    total = got_ref[0].astype(F32)
    for b in range(1, got_ref.shape[0]):
        total += got_ref[b].astype(F32)
    leaf_local = total.astype(BF16)
    for i in range(2):
        acc[i] = dot(leaf_local[:, 64 * i : 64 * (i + 1)], basis_ref[i])
    for s in range(8):
        start = pl.multiple_of(cols_ref[s] * 256, 256)
        acc[rows_ref[s]] += dot(x_ref[:, pl.ds(start, 256)], near_ref[s])
    for i in range(2):
        out_ref[:, 256 * i : 256 * (i + 1)] = acc[i].astype(BF16)


def local(
    columns_x,
    col_basis,
    col_links,
    col_top_links,
    row_basis,
    row_links,
    coupling,
    coupling_rows,
    coupling_cols,
    near_blocks,
    near_rows,
    near_cols,
):
    message = pl.pallas_call(
        moments_kernel,
        out_shape=jax.ShapeDtypeStruct((32, 48, 128), BF16),
        in_specs=[vmem()] * 3,
        out_specs=vmem(),
        name="moments",
    )(columns_x, col_basis, col_links.reshape(2, 64, 64))
    gathered = lax.all_to_all(message, "row", 0, 0)
    partials = pl.pallas_call(
        tree_kernel,
        out_shape=jax.ShapeDtypeStruct((16, 32, 128), BF16),
        in_specs=[smem()] * 2 + [vmem()] * 4,
        out_specs=vmem(),
        scratch_shapes=[pltpu.VMEM((120, 32, 64), BF16), pltpu.VMEM((60, 32, 64), F32)],
        compiler_params=pltpu.CompilerParams(vmem_limit_bytes=32 * 1024 * 1024),
        name="trees",
    )(
        coupling_rows,
        coupling_cols,
        gathered,
        col_top_links[0].reshape(48, 64, 64),
        coupling.reshape(128, 64, 64),
        row_links[0].reshape(56, 64, 64),
    )
    scattered = lax.all_to_all(partials, "col", 0, 0)
    return pl.pallas_call(
        output_kernel,
        out_shape=jax.ShapeDtypeStruct((32, 512), BF16),
        in_specs=[smem()] * 2 + [vmem()] * 4,
        out_specs=vmem(),
        scratch_shapes=[pltpu.VMEM((2, 32, 256), F32)],
        compiler_params=pltpu.CompilerParams(vmem_limit_bytes=16 * 1024 * 1024),
        name="outputs",
    )(near_rows, near_cols, scattered, row_basis, columns_x, near_blocks)


def solution(mesh):
    in_specs = (
        P(None, ("row", "col")),
        P(("row", "col"), None, None),
        P(("row", "col"), None),
        P("col", None, None),
        P(("row", "col"), None, None),
        P("row", None, None),
        P(("row", "col"), None),
        P(("row", "col"), None),
        P(("row", "col"), None),
        P(("row", "col"), None, None),
        P(("row", "col")),
        P(("row", "col")),
    )
    out_specs = P(None, ("row", "col"))
    return jax.shard_map(local, mesh=mesh, in_specs=in_specs, out_specs=out_specs, check_vma=False)
```

time: 214 us -> 55.6 us (0.26)
  the two profiles are of different devices: /device:TPU:2 before, /device:TPU:32 now
where the time goes in v1:
time: 55.6 us; the launch traced here: 55.2 us
  blocking collectives  28.9 us (52%)
  local copies, waits for them, and re-layouts  10.9 us (20%)
  starting transfers between devices  7.32 us (13%)
  Pallas kernels  5.96 us (11%)
  waiting for transfers between devices  2.03 us (4%)
    all_to_all x1, blocking collectives, local(): scattered = lax.all_to_all(partials, 'col', 0, 0)  28.9 us
    all_to_all x1, starting transfers between devices, local(): gathered = lax.all_to_all(message, 'row', 0, 0)  7.32 us
    reshape x1, local copies, waits for them, and re-layouts, local(): coupling.reshape(128, 64, 64)  2.99 us
    another operation x1, local copies, waits for them, and re-layouts, local(): col_top_links[0].reshape(48, 64, 64)  2.64 us
    pallas_call x1, Pallas kernels, local(): pl.pallas_call(tree_kernel, out_shape=jax.ShapeDtypeStruct((16, 32, 128),...  2.49 us
    all_to_all x1, waiting for transfers between devices, local(): gathered = lax.all_to_all(message, 'row', 0, 0)  2.03 us
    another operation x1, local copies, waits for them, and re-layouts, local(): row_links[0].reshape(56, 64, 64)  1.94 us
    pallas_call x1, Pallas kernels, local(): pl.pallas_call(moments_kernel, out_shape=jax.ShapeDtypeStruct((32, 48, 12...  1.93 us
  transfers between devices with their start and end apart: 1, of which 1 were waited for; matrix products, arithmetic and copies ran while one was open for 15% of the time, Pallas kernels for 0%

profile of v1, /device:TPU:32, one launch (start us, length us, event | category | flops | bytes accessed | tf_op | source)
XLA Modules:
  0.0 55.2 jit_solution(11031674602126591769)
XLA Ops:
  0.0 0.0 copy-start.8
  0.0 1.5 %reshape.6.links_ref = bf16[2,64,64]{2,1,0:T(8,128)(2,1)} reshape(bf16[2,4096]{1,0:T(2,128)(2,1)} %param.14) | data formatting | bytes 32768 | tf_op jit(solution)/shard_map/reshape | solution.py:110
  1.5 1.9 %moments.1 = bf16[32,48,128]{2,1,0:T(8,128)(2,1)} custom-call(bf16[32,512]{1,0:T(8,128)(2,1)} %x_ref.3, bf16[2,64,256]{2,1,0:T(8,128)(2,1)} %basis_ref.2, bf16[2,64,64]{2,1,0:T(8,128)(2,1)} %reshape.6.links_ref), custom_call_target="tpu_custom_call" | custom-call | tf_op jit(solution)/shard_map/moments/pallas_call | solution.py:104
  3.4 7.3 %all-to-all-start = ((bf16[32,48,128]{2,1,0:T(8,128)(2,1)}), bf16[32,48,128]{2,1,0:T(8,128)(2,1)S(1)}, u32[]{:S(2)}, u32[]{:S(2)}) async-start(bf16[32,48,128]{2,1,0:T(8,128)(2,1)} %moments.1), calls=%async_computation | async-start | bytes 786432 | tf_op jit(solution)/shard_map/all_to_all | solution.py:111
  10.8 2.6 %reshape_squeeze.6.top_ref = bf16[48,64,64]{2,1,0:T(8,128)(2,1)} reshape(bf16[1,48,4096]{2,1,0:T(8,128)(2,1)} %param.15) | data formatting | bytes 786432 | tf_op jit(solution)/shard_map/reshape;squeeze | solution.py:124
  13.4 0.0 copy-done.8
  13.4 0.7 %copy.13 = bf16[128,4096]{0,1:T(8,128)(2,1)S(1)} copy(bf16[128,4096]{1,0:T(8,128)(2,1)S(1)} %copy-done.8) | data formatting | bytes 2097152 | tf_op args[6]
  14.1 0.0 copy-start.4
  14.1 0.0 copy-start.5
  14.1 3.0 %copy.14.coupling_ref = bf16[128,64,64]{2,1,0:T(8,128)(2,1)S(1)} copy(bf16[128,64,64]{0,2,1:T(8,128)(2,1)S(1)} %bitcast.1) | data formatting | bytes 2097152 | tf_op jit(solution)/shard_map/reshape | solution.py:125
  17.1 1.9 %reshape_squeeze.7.links_ref = bf16[56,64,64]{2,1,0:T(8,128)(2,1)S(1)} reshape(bf16[1,56,4096]{2,1,0:T(8,128)(2,1)} %param.17) | data formatting | bytes 917504 | tf_op jit(solution)/shard_map/reshape;squeeze | solution.py:126
  19.1 2.0 %all-to-all-done.got_ref = bf16[32,48,128]{2,1,0:T(8,128)(2,1)S(1)} async-done(((bf16[32,48,128]{2,1,0:T(8,128)(2,1)}), bf16[32,48,128]{2,1,0:T(8,128)(2,1)S(1)}, u32[]{:S(2)}, u32[]{:S(2)}) %all-to-all-start) | async-done | bytes 393248 | tf_op jit(solution)/shard_map/all_to_all | solution.py:111
  21.1 0.0 copy-done.4
  21.1 0.0 copy-done.5
  21.1 0.0 copy-start
  21.1 1.1 %copy-done = bf16[48,64,64]{2,1,0:T(8,128)(2,1)S(1)} copy-done((bf16[48,64,64]{2,1,0:T(8,128)(2,1)S(1)}, bf16[48,64,64]{2,1,0:T(8,128)(2,1)}, u32[]{:S(2)}) %copy-start) | copy-done | bytes 393240
  22.2 0.0 copy-start.1
  22.2 0.0 copy-start.2
  22.2 0.0 copy-start.3
  22.2 0.0 copy-start.6
  22.2 0.0 copy-start.7
  22.2 2.5 %trees.1 = bf16[16,32,128]{2,1,0:T(8,128)(2,1)S(1)} custom-call(s32[4,32]{1,0:T(4,128)S(1)} %copy-done.4, s32[4,32]{1,0:T(4,128)S(1)} %copy-done.5, bf16[32,48,128]{2,1,0:T(8,128)(2,1)S(1)} %all-to-all-done.got_ref, bf16[48,64,64]{2,1,0:T(8,128)(2,1)S(1)} %copy-done, bf16[128,64,64]{2,1,0:T(8,128)(2,1)S(1)} %copy.14.coupling_ref, ...), custom_call_target="tpu_custom_call" | custom-call | tf_op jit(solution)/shard_map/trees/pallas_call | solution.py:112
  24.7 28.9 %all_to_all.10.got_ref = bf16[16,32,128]{2,1,0:T(8,128)(2,1)S(1)} all-to-all(bf16[16,32,128]{2,1,0:T(8,128)(2,1)S(1)} %trees.1), channel_id=1, replica_groups=mesh['row'=32,'col'=16] {'col'}, dimensions={0} | all-to-all | bytes 262144 | tf_op jit(solution)/shard_map/all_to_all | solution.py:128
  53.6 0.0 copy-done.1
  53.6 0.0 copy-done.2
  53.6 0.0 copy-done.3
  53.6 0.0 copy-done.6
  53.6 0.0 copy-done.7
  53.7 1.5 %outputs.1 = bf16[32,512]{1,0:T(8,128)(2,1)} custom-call(s32[8]{0:T(128)S(1)} %copy-done.6, s32[8]{0:T(128)S(1)} %copy-done.7, bf16[16,32,128]{2,1,0:T(8,128)(2,1)S(1)} %all_to_all.10.got_ref, bf16[2,64,256]{2,1,0:T(8,128)(2,1)S(1)} %copy-done.3, bf16[32,512]{1,0:T(8,128)(2,1)S(1)} %copy-done.2, bf16[8,256,256]{2,1,0:T(8,128)(2,1)S(1)} %copy-done.1), custom_call_target="tpu_custom_call" | custom-call | tf_op jit(solution)/shard_map/outputs/pallas_call | solution.py:129
Async XLA Ops:
  0.0 13.4 %copy-start.8 = (bf16[128,4096]{1,0:T(8,128)(2,1)S(1)}, bf16[128,4096]{1,0:T(8,128)(2,1)}, u32[]{:S(2)}) copy-start(bf16[128,4096]{1,0:T(8,128)(2,1)} %param.18) | copy-start | bytes 3145732
  3.4 17.6 %all-to-all-start = ((bf16[32,48,128]{2,1,0:T(8,128)(2,1)}), bf16[32,48,128]{2,1,0:T(8,128)(2,1)S(1)}, u32[]{:S(2)}, u32[]{:S(2)}) async-start(bf16[32,48,128]{2,1,0:T(8,128)(2,1)} %moments.1), calls=%async_computation | async-start | bytes 786432 | tf_op jit(solution)/shard_map/all_to_all | solution.py:111
  14.1 7.0 %copy-start.4 = (s32[4,32]{1,0:T(4,128)S(1)}, s32[4,32]{1,0:T(4,128)}, u32[]{:S(2)}) copy-start(s32[4,32]{1,0:T(4,128)} %rows_ref.2) | copy-start | bytes 1540
  14.1 7.0 %copy-start.5 = (s32[4,32]{1,0:T(4,128)S(1)}, s32[4,32]{1,0:T(4,128)}, u32[]{:S(2)}) copy-start(s32[4,32]{1,0:T(4,128)} %cols_ref.2) | copy-start | bytes 1540
  21.1 1.1 %copy-start = (bf16[48,64,64]{2,1,0:T(8,128)(2,1)S(1)}, bf16[48,64,64]{2,1,0:T(8,128)(2,1)}, u32[]{:S(2)}) copy-start(bf16[48,64,64]{2,1,0:T(8,128)(2,1)} %reshape_squeeze.6.top_ref) | copy-start | bytes 1179652
  22.2 31.4 %copy-start.1 = (bf16[8,256,256]{2,1,0:T(8,128)(2,1)S(1)}, bf16[8,256,256]{2,1,0:T(8,128)(2,1)}, u32[]{:S(2)}) copy-start(bf16[8,256,256]{2,1,0:T(8,128)(2,1)} %near_ref.1) | copy-start | bytes 3145732
  22.2 31.4 %copy-start.2 = (bf16[32,512]{1,0:T(8,128)(2,1)S(1)}, bf16[32,512]{1,0:T(8,128)(2,1)}, u32[]{:S(2)}) copy-start(bf16[32,512]{1,0:T(8,128)(2,1)} %x_ref.3) | copy-start | bytes 98308
  22.2 31.4 %copy-start.3 = (bf16[2,64,256]{2,1,0:T(8,128)(2,1)S(1)}, bf16[2,64,256]{2,1,0:T(8,128)(2,1)}, u32[]{:S(2)}) copy-start(bf16[2,64,256]{2,1,0:T(8,128)(2,1)} %basis_ref.3) | copy-start | bytes 196612
  22.2 31.4 %copy-start.6 = (s32[8]{0:T(128)S(1)}, s32[8]{0:T(128)}, u32[]{:S(2)}) copy-start(s32[8]{0:T(128)} %rows_ref.3) | copy-start | bytes 100
  22.2 31.4 %copy-start.7 = (s32[8]{0:T(128)S(1)}, s32[8]{0:T(128)}, u32[]{:S(2)}) copy-start(s32[8]{0:T(128)} %cols_ref.3) | copy-start | bytes 100

commit v2 on v1

v2 whole, which is shorter than its diff:
```python
import jax
import jax.numpy as jnp
from jax import lax
from jax.experimental import pallas as pl
from jax.experimental.pallas import tpu as pltpu
from jax.sharding import PartitionSpec as P

F32 = jnp.float32
BF16 = jnp.bfloat16


def dot(a, b):
    return jnp.dot(a, b, preferred_element_type=F32)


def vmem():
    return pl.BlockSpec(memory_space=pltpu.VMEM)


def smem():
    return pl.BlockSpec(memory_space=pltpu.SMEM)


def out_vmem(shape, dtype):
    return pltpu.VMEM(shape, dtype)


def moments_kernel(x_ref, basis_ref, links_ref, out_ref):
    links = links_ref[...].reshape(2, 64, 64)
    leaves = []
    for i in range(2):
        moment = lax.dot_general(
            x_ref[:, 256 * i : 256 * (i + 1)],
            basis_ref[i],
            (((1,), (1,)), ((), ())),
            preferred_element_type=F32,
        )
        leaves.append(moment.astype(BF16))
    parent = dot(leaves[0], links[0]) + dot(leaves[1], links[1])
    low = jnp.concatenate(leaves, axis=1)
    high = jnp.concatenate([parent[:16], parent[16:]], axis=1).astype(BF16)
    for r in range(out_ref.shape[0]):
        out_ref[r, 0:32, :] = low
        out_ref[r, 32:48, :] = high


def beside(matrices):
    half = matrices.shape[0] // 2
    return jnp.concatenate([matrices[:half], matrices[half:]], axis=2)


def matrix(ref, j):
    side, place = divmod(j, ref.shape[0])
    return ref[place, :, 64 * side : 64 * (side + 1)]


def unpack_kernel(coupling_ref, top_ref, links_ref, rows_ref, cols_ref, blocks_ref, up_ref, down_ref, lists_ref):
    lists_ref[0:4, 0:32] = rows_ref[...]
    lists_ref[4:8, 0:32] = cols_ref[...]
    blocks_ref[...] = beside(coupling_ref[...].reshape(128, 64, 64))
    up_ref[...] = beside(top_ref[0].reshape(48, 64, 64))
    down_ref[...] = beside(links_ref[0].reshape(56, 64, 64))


def tree_kernel(
    lists_in, got_ref, top_ref, coupling_ref, links_ref, out_ref,
    mom0, mom1, mom2, mom3, acc0, acc1, acc2, acc3, lists_ref, sem,
):
    mom, acc = (mom0, mom1, mom2, mom3), (acc0, acc1, acc2, acc3)
    copy = pltpu.make_async_copy(lists_in, lists_ref, sem)
    copy.start()
    for a in range(32):
        both = got_ref[a, 0:32, :]
        mom0[2 * a] = both[:, 0:64]
        mom0[2 * a + 1] = both[:, 64:128]
        parent = got_ref[a, 32:48, :]
        mom1[a, 0:16] = parent[:, 0:64]
        mom1[a, 16:32] = parent[:, 64:128]
    for depth in range(4):
        acc[depth][...] = jnp.zeros_like(acc[depth])
    for p in range(16):
        mom2[p] = (dot(mom1[2 * p], matrix(top_ref, 2 * p)) + dot(mom1[2 * p + 1], matrix(top_ref, 2 * p + 1))).astype(BF16)
    for p in range(8):
        mom3[p] = (dot(mom2[2 * p], matrix(top_ref, 32 + 2 * p)) + dot(mom2[2 * p + 1], matrix(top_ref, 33 + 2 * p))).astype(BF16)
    copy.wait()
    for s in range(32):
        for depth in range(4):
            q, p = lists_ref[4 + depth, s], lists_ref[depth, s]
            acc[depth][p] += dot(mom[depth][q], matrix(coupling_ref, depth * 32 + s))
    for depth in (2, 1, 0):
        count = 32 >> depth
        start = 2 * (32 - count)
        for p in range(count):
            acc[depth][p] += dot(acc[depth + 1][p // 2].astype(BF16), matrix(links_ref, start + p))
    for b in range(16):
        out_ref[b, :, 0:64] = acc0[2 * b].astype(BF16)
        out_ref[b, :, 64:128] = acc0[2 * b + 1].astype(BF16)


def near_kernel(rows_ref, cols_ref, x_ref, near_ref, out_ref):
    out_ref[...] = jnp.zeros_like(out_ref)
    for s in range(8):
        start = pl.multiple_of(cols_ref[s] * 256, 256)
        out_ref[rows_ref[s]] += dot(x_ref[:, pl.ds(start, 256)], near_ref[s])


def output_kernel(got_ref, basis_ref, near_ref, out_ref):
    total = got_ref[0].astype(F32)
    for b in range(1, got_ref.shape[0]):
        total += got_ref[b].astype(F32)
    leaf_local = total.astype(BF16)
    for i in range(2):
        distant = dot(leaf_local[:, 64 * i : 64 * (i + 1)], basis_ref[i])
        out_ref[:, 256 * i : 256 * (i + 1)] = (distant + near_ref[i]).astype(BF16)


def local(
    columns_x,
    col_basis,
    col_links,
    col_top_links,
    row_basis,
    row_links,
    coupling,
    coupling_rows,
    coupling_cols,
    near_blocks,
    near_rows,
    near_cols,
):
    message = pl.pallas_call(
        moments_kernel,
        out_shape=jax.ShapeDtypeStruct((32, 48, 128), BF16),
        in_specs=[vmem()] * 3,
        out_specs=vmem(),
        name="moments",
    )(columns_x, col_basis, col_links)
    gathered = lax.all_to_all(message, "row", 0, 0)
    blocks, up, down, lists = pl.pallas_call(
        unpack_kernel,
        out_shape=[out_vmem((count, 64, 128), BF16) for count in (64, 24, 28)] + [out_vmem((8, 128), jnp.int32)],
        in_specs=[vmem()] * 5,
        out_specs=[vmem()] * 4,
        compiler_params=pltpu.CompilerParams(vmem_limit_bytes=16 * 1024 * 1024),
        cost_estimate=pl.CostEstimate(flops=0, bytes_accessed=8_000_000, transcendentals=0),
        name="unpack",
    )(coupling, col_top_links, row_links, coupling_rows, coupling_cols)
    nearby = pl.pallas_call(
        near_kernel,
        out_shape=out_vmem((2, 32, 256), F32),
        in_specs=[smem()] * 2 + [vmem()] * 2,
        out_specs=vmem(),
        compiler_params=pltpu.CompilerParams(vmem_limit_bytes=16 * 1024 * 1024),
        cost_estimate=pl.CostEstimate(flops=33_554_432, bytes_accessed=1_200_000, transcendentals=0),
        name="near",
    )(near_rows, near_cols, columns_x, near_blocks)
    partials = pl.pallas_call(
        tree_kernel,
        out_shape=jax.ShapeDtypeStruct((16, 32, 128), BF16),
        in_specs=[vmem()] * 5,
        out_specs=vmem(),
        scratch_shapes=[pltpu.VMEM((64 >> depth, 32, 64), BF16) for depth in range(4)]
        + [pltpu.VMEM((32 >> depth, 32, 64), F32) for depth in range(4)]
        + [pltpu.SMEM((8, 128), jnp.int32), pltpu.SemaphoreType.DMA],
        compiler_params=pltpu.CompilerParams(vmem_limit_bytes=16 * 1024 * 1024),
        name="trees",
    )(lists, gathered, up, blocks, down)
    scattered = lax.all_to_all(partials, "col", 0, 0)
    return pl.pallas_call(
        output_kernel,
        out_shape=jax.ShapeDtypeStruct((32, 512), BF16),
        in_specs=[vmem()] * 3,
        out_specs=vmem(),
        compiler_params=pltpu.CompilerParams(vmem_limit_bytes=8 * 1024 * 1024),
        name="outputs",
    )(scattered, row_basis, nearby)


def solution(mesh):
    in_specs = (
        P(None, ("row", "col")),
        P(("row", "col"), None, None),
        P(("row", "col"), None),
        P("col", None, None),
        P(("row", "col"), None, None),
        P("row", None, None),
        P(("row", "col"), None),
        P(("row", "col"), None),
        P(("row", "col"), None),
        P(("row", "col"), None, None),
        P(("row", "col")),
        P(("row", "col")),
    )
    out_specs = P(None, ("row", "col"))
    return jax.shard_map(local, mesh=mesh, in_specs=in_specs, out_specs=out_specs, check_vma=False)
```

time: 55.6 us -> 53.1 us (0.955)
  blocking collectives: 28.9 us -> 0 us
  waiting for transfers between devices: 2.03 us -> 19.7 us
  starting transfers between devices: 7.32 us -> 22.8 us
  local copies, waits for them, and re-layouts: 10.9 us -> 2.05 us
  Pallas kernels: 5.96 us -> 7.98 us
    all_to_all x1 -> x0, blocking collectives: 28.9 us -> none  [local(): scattered = lax.all_to_all(partials, 'col', 0, 0)]
    all_to_all x0 -> x1, starting transfers between devices: none -> 15.4 us  [local(): scattered = lax.all_to_all(partials, 'col', 0, 0)]
    all_to_all x0 -> x1, waiting for transfers between devices: none -> 13.1 us  [local(): scattered = lax.all_to_all(partials, 'col', 0, 0)]
    all_to_all x1, waiting for transfers between devices: 2.03 us -> 6.65 us  [local(): gathered = lax.all_to_all(message, 'row', 0, 0)]
    another operation x2 -> x0, local copies, waits for them, and re-layouts: 4.58 us -> none  [the longest x1 2.64 us: local(): col_top_links[0].reshape(48, 64, 64)]
    reshape x2 -> x0, local copies, waits for them, and re-layouts: 4.5 us -> none  [the longest x1 2.99 us: local(): coupling.reshape(128, 64, 64)]
    pallas_call x0 -> x2, Pallas kernels: none -> 2.44 us  [the longest x1 1.6 us: local(): pl.pallas_call(unpack_kernel, out_shape=[out_vmem((count, 64, 128), BF16)...]
    pallas_call x1, Pallas kernels: 1.54 us -> 0.83 us  [local(): pl.pallas_call(output_kernel, out_shape=jax.ShapeDtypeStruct((32, 512), B...]
  transfers between devices with their start and end apart: 1 -> 2, of which waited for: 1 -> 2; matrix products, arithmetic and copies ran while one was open for 15% -> 0% of each run, Pallas kernels for 0% -> 5%
where the time goes in v2:
time: 53.1 us; the launch traced here: 52.7 us
  starting transfers between devices  22.8 us (43%)
  waiting for transfers between devices  19.7 us (37%)
  Pallas kernels  7.98 us (15%)
  local copies, waits for them, and re-layouts  2.05 us (4%)
    all_to_all x1, starting transfers between devices, local(): scattered = lax.all_to_all(partials, 'col', 0, 0)  15.4 us
    all_to_all x1, waiting for transfers between devices, local(): scattered = lax.all_to_all(partials, 'col', 0, 0)  13.1 us
    all_to_all x1, starting transfers between devices, local(): gathered = lax.all_to_all(message, 'row', 0, 0)  7.45 us
    all_to_all x1, waiting for transfers between devices, local(): gathered = lax.all_to_all(message, 'row', 0, 0)  6.65 us
    pallas_call x1, Pallas kernels, local(): pl.pallas_call(tree_kernel, out_shape=jax.ShapeDtypeStruct((16, 32, 128),...  2.72 us
    unnamed x20, local copies, waits for them, and re-layouts  2.05 us
    pallas_call x1, Pallas kernels, local(): pl.pallas_call(moments_kernel, out_shape=jax.ShapeDtypeStruct((32, 48, 12...  2 us
    pallas_call x1, Pallas kernels, local(): pl.pallas_call(unpack_kernel, out_shape=[out_vmem((count, 64, 128), BF16)...  1.6 us
  transfers between devices with their start and end apart: 2, of which 2 were waited for; matrix products, arithmetic and copies ran while one was open for 0% of the time, Pallas kernels for 5%

profile of v2, /device:TPU:32, one launch (start us, length us, event | category | flops | bytes accessed | tf_op | source)
XLA Modules:
  0.0 52.7 jit_solution(16144264641344488065)
XLA Ops:
  0.0 0.0 copy-start
  0.0 2.0 %moments.1 = bf16[32,48,128]{2,1,0:T(8,128)(2,1)} custom-call(bf16[32,512]{1,0:T(8,128)(2,1)} %x_ref.3, bf16[2,64,256]{2,1,0:T(8,128)(2,1)} %basis_ref.2, bf16[2,4096]{1,0:T(2,128)(2,1)} %links_ref.3), custom_call_target="tpu_custom_call" | custom-call | tf_op jit(solution)/shard_map/moments/pallas_call | solution.py:131
  2.0 0.0 copy-start.6
  2.0 0.0 copy-start.7
  2.0 7.5 %all-to-all-start = ((bf16[32,48,128]{2,1,0:T(8,128)(2,1)}), bf16[32,48,128]{2,1,0:T(8,128)(2,1)S(1)}, u32[]{:S(2)}, u32[]{:S(2)}) async-start(bf16[32,48,128]{2,1,0:T(8,128)(2,1)} %moments.1), calls=%async_computation | async-start | bytes 786432 | tf_op jit(solution)/shard_map/all_to_all | solution.py:138
  9.5 0.0 copy-done
  9.5 0.0 copy-done.6
  9.5 0.0 copy-done.7
  9.5 0.0 copy-start.2
  9.5 1.0 %copy-done.2 = bf16[1,56,4096]{2,1,0:T(8,128)(2,1)S(1)} copy-done((bf16[1,56,4096]{2,1,0:T(8,128)(2,1)S(1)}, bf16[1,56,4096]{2,1,0:T(8,128)(2,1)}, u32[]{:S(2)}) %copy-start.2) | copy-done | bytes 458776
  10.5 0.0 copy-start.3
  10.5 1.0 %copy-done.3 = bf16[1,48,4096]{2,1,0:T(8,128)(2,1)S(1)} copy-done((bf16[1,48,4096]{2,1,0:T(8,128)(2,1)S(1)}, bf16[1,48,4096]{2,1,0:T(8,128)(2,1)}, u32[]{:S(2)}) %copy-start.3) | copy-done | bytes 393240
  11.5 1.6 %unpack.1 = (bf16[64,64,128]{2,1,0:T(8,128)(2,1)S(1)}, bf16[24,64,128]{2,1,0:T(8,128)(2,1)S(1)}, bf16[28,64,128]{2,1,0:T(8,128)(2,1)S(1)}, s32[8,128]{1,0:T(8,128)S(1)}) custom-call(bf16[128,4096]{1,0:T(8,128)(2,1)S(1)} %copy-done, bf16[1,48,4096]{2,1,0:T(8,128)(2,1)S(1)} %copy-done.3, bf16[1,56,4096]{2,1,0:T(8,128)(2,1)S(1)} %copy-done.2, ...), custom_call_target="tpu_custom_call" | custom-call | bytes 8000000 | tf_op jit(solution)/shard_map/unpack/pallas_call | solution.py:139
  13.1 6.7 %all-to-all-done.got_ref = bf16[32,48,128]{2,1,0:T(8,128)(2,1)S(1)} async-done(((bf16[32,48,128]{2,1,0:T(8,128)(2,1)}), bf16[32,48,128]{2,1,0:T(8,128)(2,1)S(1)}, u32[]{:S(2)}, u32[]{:S(2)}) %all-to-all-start) | async-done | bytes 393248 | tf_op jit(solution)/shard_map/all_to_all | solution.py:138
  19.8 0.0 copy-start.1
  19.8 2.7 %trees.1 = bf16[16,32,128]{2,1,0:T(8,128)(2,1)} custom-call(s32[8,128]{1,0:T(8,128)S(1)} %get-tuple-element.9.lists_in, bf16[32,48,128]{2,1,0:T(8,128)(2,1)S(1)} %all-to-all-done.got_ref, bf16[24,64,128]{2,1,0:T(8,128)(2,1)S(1)} %get-tuple-element.10.top_ref, bf16[64,64,128]{2,1,0:T(8,128)(2,1)S(1)} %get-tuple-element.11.coupling_ref, ...), custom_call_target="tpu_custom_call" | custom-call | tf_op jit(solution)/shard_map/trees/pallas_call | solution.py:157
  22.5 0.0 copy-start.4
  22.5 0.0 copy-start.8
  22.5 0.0 copy-start.9
  22.5 15.4 %all-to-all-start.1 = ((bf16[16,32,128]{2,1,0:T(8,128)(2,1)}), bf16[16,32,128]{2,1,0:T(8,128)(2,1)S(1)}, u32[]{:S(2)}, u32[]{:S(2)}) async-start(bf16[16,32,128]{2,1,0:T(8,128)(2,1)} %trees.1), calls=%async_computation.1 | async-start | bytes 262144 | tf_op jit(solution)/shard_map/all_to_all | solution.py:168
  37.9 0.0 copy-done.1
  37.9 0.0 copy-done.4
  37.9 0.0 copy-done.8
  37.9 0.0 copy-done.9
  37.9 0.0 copy-start.5
  37.9 0.8 %near.1.near_ref = f32[2,32,256]{2,1,0:T(8,128)S(1)} custom-call(s32[8]{0:T(128)S(1)} %copy-done.8, s32[8]{0:T(128)S(1)} %copy-done.9, bf16[32,512]{1,0:T(8,128)(2,1)S(1)} %copy-done.4, bf16[8,256,256]{2,1,0:T(8,128)(2,1)S(1)} %copy-done.1), custom_call_target="tpu_custom_call" | custom-call | flops 33554432 | bytes 1200000 | tf_op jit(solution)/shard_map/near/pallas_call | solution.py:148
  38.8 13.1 %all-to-all-done.1.got_ref = bf16[16,32,128]{2,1,0:T(8,128)(2,1)S(1)} async-done(((bf16[16,32,128]{2,1,0:T(8,128)(2,1)}), bf16[16,32,128]{2,1,0:T(8,128)(2,1)S(1)}, u32[]{:S(2)}, u32[]{:S(2)}) %all-to-all-start.1) | async-done | bytes 131104 | tf_op jit(solution)/shard_map/all_to_all | solution.py:168
  51.8 0.0 copy-done.5
  51.8 0.8 %outputs.1 = bf16[32,512]{1,0:T(8,128)(2,1)} custom-call(bf16[16,32,128]{2,1,0:T(8,128)(2,1)S(1)} %all-to-all-done.1.got_ref, bf16[2,64,256]{2,1,0:T(8,128)(2,1)S(1)} %copy-done.5, f32[2,32,256]{2,1,0:T(8,128)S(1)} %near.1.near_ref), custom_call_target="tpu_custom_call" | custom-call | tf_op jit(solution)/shard_map/outputs/pallas_call | solution.py:169
Async XLA Ops:
  0.0 9.5 %copy-start = (bf16[128,4096]{1,0:T(8,128)(2,1)S(1)}, bf16[128,4096]{1,0:T(8,128)(2,1)}, u32[]{:S(2)}) copy-start(bf16[128,4096]{1,0:T(8,128)(2,1)} %coupling_ref.1) | copy-start | bytes 3145732
  2.0 7.5 %copy-start.6 = (s32[4,32]{1,0:T(4,128)S(1)}, s32[4,32]{1,0:T(4,128)}, u32[]{:S(2)}) copy-start(s32[4,32]{1,0:T(4,128)} %rows_ref.2) | copy-start | bytes 1540
  2.0 7.5 %copy-start.7 = (s32[4,32]{1,0:T(4,128)S(1)}, s32[4,32]{1,0:T(4,128)}, u32[]{:S(2)}) copy-start(s32[4,32]{1,0:T(4,128)} %cols_ref.2) | copy-start | bytes 1540
  2.0 17.8 %all-to-all-start = ((bf16[32,48,128]{2,1,0:T(8,128)(2,1)}), bf16[32,48,128]{2,1,0:T(8,128)(2,1)S(1)}, u32[]{:S(2)}, u32[]{:S(2)}) async-start(bf16[32,48,128]{2,1,0:T(8,128)(2,1)} %moments.1), calls=%async_computation | async-start | bytes 786432 | tf_op jit(solution)/shard_map/all_to_all | solution.py:138
  9.5 1.0 %copy-start.2 = (bf16[1,56,4096]{2,1,0:T(8,128)(2,1)S(1)}, bf16[1,56,4096]{2,1,0:T(8,128)(2,1)}, u32[]{:S(2)}) copy-start(bf16[1,56,4096]{2,1,0:T(8,128)(2,1)} %links_ref.2) | copy-start | bytes 1376260
  10.5 1.0 %copy-start.3 = (bf16[1,48,4096]{2,1,0:T(8,128)(2,1)S(1)}, bf16[1,48,4096]{2,1,0:T(8,128)(2,1)}, u32[]{:S(2)}) copy-start(bf16[1,48,4096]{2,1,0:T(8,128)(2,1)} %top_ref.1) | copy-start | bytes 1179652
  19.8 18.1 %copy-start.1 = (bf16[8,256,256]{2,1,0:T(8,128)(2,1)S(1)}, bf16[8,256,256]{2,1,0:T(8,128)(2,1)}, u32[]{:S(2)}) copy-start(bf16[8,256,256]{2,1,0:T(8,128)(2,1)} %near_ref.1) | copy-start | bytes 3145732
  22.5 15.4 %copy-start.4 = (bf16[32,512]{1,0:T(8,128)(2,1)S(1)}, bf16[32,512]{1,0:T(8,128)(2,1)}, u32[]{:S(2)}) copy-start(bf16[32,512]{1,0:T(8,128)(2,1)} %x_ref.3) | copy-start | bytes 98308
  22.5 15.4 %copy-start.8 = (s32[8]{0:T(128)S(1)}, s32[8]{0:T(128)}, u32[]{:S(2)}) copy-start(s32[8]{0:T(128)} %rows_ref.3) | copy-start | bytes 100
  22.5 15.4 %copy-start.9 = (s32[8]{0:T(128)S(1)}, s32[8]{0:T(128)}, u32[]{:S(2)}) copy-start(s32[8]{0:T(128)} %cols_ref.3) | copy-start | bytes 100
  22.5 29.3 %all-to-all-start.1 = ((bf16[16,32,128]{2,1,0:T(8,128)(2,1)}), bf16[16,32,128]{2,1,0:T(8,128)(2,1)S(1)}, u32[]{:S(2)}, u32[]{:S(2)}) async-start(bf16[16,32,128]{2,1,0:T(8,128)(2,1)} %trees.1), calls=%async_computation.1 | async-start | bytes 262144 | tf_op jit(solution)/shard_map/all_to_all | solution.py:168
  37.9 13.9 %copy-start.5 = (bf16[2,64,256]{2,1,0:T(8,128)(2,1)S(1)}, bf16[2,64,256]{2,1,0:T(8,128)(2,1)}, u32[]{:S(2)}) copy-start(bf16[2,64,256]{2,1,0:T(8,128)(2,1)} %basis_ref.3) | copy-start | bytes 196612

commit v3 on v2

--- a/solution.py
+++ b/solution.py
@@ -59,42 +59,46 @@
     lists_ref[4:8, 0:32] = cols_ref[...]
     blocks_ref[...] = beside(coupling_ref[...].reshape(128, 64, 64))
     up_ref[...] = beside(top_ref[0].reshape(48, 64, 64))
-    down_ref[...] = beside(links_ref[0].reshape(56, 64, 64))
+    links = links_ref[0].reshape(56, 64, 64)
+    for b in range(16):
+        one = jnp.concatenate([links[2 * b], links[2 * b + 1]], axis=1)
+        two = dot(links[32 + b], one).astype(BF16)
+        three = dot(links[48 + b // 2], two).astype(BF16)
+        down_ref[b, 0:64, :] = one
+        down_ref[b, 64:128, :] = two
+        down_ref[b, 128:192, :] = three
 
 
 def tree_kernel(
-    lists_in, got_ref, top_ref, coupling_ref, links_ref, out_ref,
+    lists_in, got_ref, top_ref, coupling_ref, down_ref, out_ref,
     mom0, mom1, mom2, mom3, acc0, acc1, acc2, acc3, lists_ref, sem,
 ):
     mom, acc = (mom0, mom1, mom2, mom3), (acc0, acc1, acc2, acc3)
     copy = pltpu.make_async_copy(lists_in, lists_ref, sem)
     copy.start()
     for a in range(32):
+        parent = got_ref[a, 32:48, :]
+        mom1[a, 0:16] = parent[:, 0:64]
+        mom1[a, 16:32] = parent[:, 64:128]
+    for p in range(16):
+        mom2[p] = (dot(mom1[2 * p], matrix(top_ref, 2 * p)) + dot(mom1[2 * p + 1], matrix(top_ref, 2 * p + 1))).astype(BF16)
+    for a in range(32):
         both = got_ref[a, 0:32, :]
         mom0[2 * a] = both[:, 0:64]
         mom0[2 * a + 1] = both[:, 64:128]
-        parent = got_ref[a, 32:48, :]
-        mom1[a, 0:16] = parent[:, 0:64]
-        mom1[a, 16:32] = parent[:, 64:128]
+    for p in range(8):
+        mom3[p] = (dot(mom2[2 * p], matrix(top_ref, 32 + 2 * p)) + dot(mom2[2 * p + 1], matrix(top_ref, 33 + 2 * p))).astype(BF16)
     for depth in range(4):
         acc[depth][...] = jnp.zeros_like(acc[depth])
-    for p in range(16):
-        mom2[p] = (dot(mom1[2 * p], matrix(top_ref, 2 * p)) + dot(mom1[2 * p + 1], matrix(top_ref, 2 * p + 1))).astype(BF16)
-    for p in range(8):
-        mom3[p] = (dot(mom2[2 * p], matrix(top_ref, 32 + 2 * p)) + dot(mom2[2 * p + 1], matrix(top_ref, 33 + 2 * p))).astype(BF16)
     copy.wait()
     for s in range(32):
         for depth in range(4):
             q, p = lists_ref[4 + depth, s], lists_ref[depth, s]
             acc[depth][p] += dot(mom[depth][q], matrix(coupling_ref, depth * 32 + s))
-    for depth in (2, 1, 0):
-        count = 32 >> depth
-        start = 2 * (32 - count)
-        for p in range(count):
-            acc[depth][p] += dot(acc[depth + 1][p // 2].astype(BF16), matrix(links_ref, start + p))
     for b in range(16):
-        out_ref[b, :, 0:64] = acc0[2 * b].astype(BF16)
-        out_ref[b, :, 64:128] = acc0[2 * b + 1].astype(BF16)
+        upper = jnp.concatenate([acc1[b], acc2[b // 2], acc3[b // 4]], axis=1).astype(BF16)
+        own = jnp.concatenate([acc0[2 * b], acc0[2 * b + 1]], axis=1)
+        out_ref[b] = (own + dot(upper, down_ref[b])).astype(BF16)
 
 
 def near_kernel(rows_ref, cols_ref, x_ref, near_ref, out_ref):
@@ -138,7 +142,12 @@
     gathered = lax.all_to_all(message, "row", 0, 0)
     blocks, up, down, lists = pl.pallas_call(
         unpack_kernel,
-        out_shape=[out_vmem((count, 64, 128), BF16) for count in (64, 24, 28)] + [out_vmem((8, 128), jnp.int32)],
+        out_shape=[
+            out_vmem((64, 64, 128), BF16),
+            out_vmem((24, 64, 128), BF16),
+            out_vmem((16, 192, 128), BF16),
+            out_vmem((8, 128), jnp.int32),
+        ],
         in_specs=[vmem()] * 5,
         out_specs=[vmem()] * 4,
         compiler_params=pltpu.CompilerParams(vmem_limit_bytes=16 * 1024 * 1024),
@@ -154,6 +163,7 @@
         cost_estimate=pl.CostEstimate(flops=33_554_432, bytes_accessed=1_200_000, transcendentals=0),
         name="near",
     )(near_rows, near_cols, columns_x, near_blocks)
+    gathered, nearby = lax.optimization_barrier((gathered, nearby))
     partials = pl.pallas_call(
         tree_kernel,
         out_shape=jax.ShapeDtypeStruct((16, 32, 128), BF16),

time: 53.1 us -> 52.9 us (level)
  blocking collectives: 0 us -> 29.1 us
  starting transfers between devices: 22.8 us -> 7.45 us
  waiting for transfers between devices: 19.7 us -> 5 us
  local copies, waits for them, and re-layouts: 2.05 us -> 3.79 us
  Pallas kernels: 7.98 us -> 7.1 us
    all_to_all x0 -> x1, blocking collectives: none -> 29.1 us  [local(): scattered = lax.all_to_all(partials, 'col', 0, 0)]
    all_to_all x1 -> x0, starting transfers between devices: 15.4 us -> none  [local(): scattered = lax.all_to_all(partials, 'col', 0, 0)]
    all_to_all x1 -> x0, waiting for transfers between devices: 13.1 us -> none  [local(): scattered = lax.all_to_all(partials, 'col', 0, 0)]
    unnamed x20 -> x24, local copies, waits for them, and re-layouts: 2.05 us -> 3.79 us
    all_to_all x1, waiting for transfers between devices: 6.65 us -> 5 us  [local(): gathered = lax.all_to_all(message, 'row', 0, 0)]
    pallas_call x1, Pallas kernels: 2.72 us -> 1.81 us  [local(): pl.pallas_call(tree_kernel, out_shape=jax.ShapeDtypeStruct((16, 32, 128),...]
  transfers between devices with their start and end apart: 2 -> 1, of which waited for: 2 -> 1; matrix products, arithmetic and copies ran while one was open for 0% -> 0% of each run, Pallas kernels for 5% -> 5%
where the time goes in v3:
time: 52.9 us; the launch traced here: 52.5 us
  blocking collectives  29.1 us (55%)
  starting transfers between devices  7.45 us (14%)
  Pallas kernels  7.1 us (13%)
  waiting for transfers between devices  5 us (9%)
  local copies, waits for them, and re-layouts  3.79 us (7%)
    all_to_all x1, blocking collectives, local(): scattered = lax.all_to_all(partials, 'col', 0, 0)  29.1 us
    all_to_all x1, starting transfers between devices, local(): gathered = lax.all_to_all(message, 'row', 0, 0)  7.45 us
    all_to_all x1, waiting for transfers between devices, local(): gathered = lax.all_to_all(message, 'row', 0, 0)  5 us
    unnamed x24, local copies, waits for them, and re-layouts  3.79 us
    pallas_call x1, Pallas kernels, local(): pl.pallas_call(moments_kernel, out_shape=jax.ShapeDtypeStruct((32, 48, 12...  2 us
    pallas_call x1, Pallas kernels, local(): pl.pallas_call(tree_kernel, out_shape=jax.ShapeDtypeStruct((16, 32, 128),...  1.81 us
    pallas_call x1, Pallas kernels, local(): pl.pallas_call(unpack_kernel, out_shape=[out_vmem((64, 64, 128), BF16), o...  1.63 us
  transfers between devices with their start and end apart: 1, of which 1 were waited for; matrix products, arithmetic and copies ran while one was open for 0% of the time, Pallas kernels for 5%

profile of v3, /device:TPU:32, one launch (start us, length us, event | category | flops | bytes accessed | tf_op | source)
XLA Modules:
  0.0 52.5 jit_solution(7463807031683413058)
XLA Ops:
  0.0 0.0 copy-start
  0.0 2.0 %moments.1 = bf16[32,48,128]{2,1,0:T(8,128)(2,1)} custom-call(bf16[32,512]{1,0:T(8,128)(2,1)} %x_ref.3, bf16[2,64,256]{2,1,0:T(8,128)(2,1)} %basis_ref.2, bf16[2,4096]{1,0:T(2,128)(2,1)} %links_ref.3), custom_call_target="tpu_custom_call" | custom-call | tf_op jit(solution)/shard_map/moments/pallas_call | solution.py:135
  2.0 0.0 copy-start.8
  2.0 0.0 copy-start.9
  2.0 7.5 %all-to-all-start = ((bf16[32,48,128]{2,1,0:T(8,128)(2,1)}), bf16[32,48,128]{2,1,0:T(8,128)(2,1)S(1)}, u32[]{:S(2)}, u32[]{:S(2)}) async-start(bf16[32,48,128]{2,1,0:T(8,128)(2,1)} %moments.1), calls=%async_computation | async-start | bytes 786432 | tf_op jit(solution)/shard_map/all_to_all | solution.py:142
  9.5 0.0 copy-done
  9.5 0.0 copy-done.8
  9.5 0.0 copy-done.9
  9.5 0.0 copy-start.2
  9.5 1.0 %copy-done.2 = bf16[1,56,4096]{2,1,0:T(8,128)(2,1)S(1)} copy-done((bf16[1,56,4096]{2,1,0:T(8,128)(2,1)S(1)}, bf16[1,56,4096]{2,1,0:T(8,128)(2,1)}, u32[]{:S(2)}) %copy-start.2) | copy-done | bytes 458776
  10.5 0.0 copy-start.3
  10.5 1.0 %copy-done.3 = bf16[1,48,4096]{2,1,0:T(8,128)(2,1)S(1)} copy-done((bf16[1,48,4096]{2,1,0:T(8,128)(2,1)S(1)}, bf16[1,48,4096]{2,1,0:T(8,128)(2,1)}, u32[]{:S(2)}) %copy-start.3) | copy-done | bytes 393240
  11.5 0.0 copy-start.1
  11.5 0.0 copy-start.6
  11.5 0.0 copy-start.10
  11.5 0.0 copy-start.11
  11.5 1.6 %unpack.1 = (bf16[64,64,128]{2,1,0:T(8,128)(2,1)S(1)}, bf16[24,64,128]{2,1,0:T(8,128)(2,1)S(1)}, bf16[16,192,128]{2,1,0:T(8,128)(2,1)S(1)}, s32[8,128]{1,0:T(8,128)S(1)}) custom-call(bf16[128,4096]{1,0:T(8,128)(2,1)S(1)} %copy-done, bf16[1,48,4096]{2,1,0:T(8,128)(2,1)S(1)} %copy-done.3, bf16[1,56,4096]{2,1,0:T(8,128)(2,1)S(1)} %copy-done.2, ...), custom_call_target="tpu_custom_call" | custom-call | bytes 8000000 | tf_op jit(solution)/shard_map/unpack/pallas_call | solution.py:143
  13.2 0.0 copy-start.4
  13.2 0.8 %copy-done.4 = bf16[24,64,128]{2,1,0:T(8,128)(2,1)} copy-done((bf16[24,64,128]{2,1,0:T(8,128)(2,1)}, bf16[24,64,128]{2,1,0:T(8,128)(2,1)S(1)}, u32[]{:S(2)}) %copy-start.4) | copy-done | bytes 393240
  13.9 0.0 copy-done.1
  13.9 0.0 copy-done.6
  13.9 0.0 copy-done.10
  13.9 0.0 copy-done.11
  13.9 0.8 %near.1.near_ref = f32[2,32,256]{2,1,0:T(8,128)S(1)} custom-call(s32[8]{0:T(128)S(1)} %copy-done.10, s32[8]{0:T(128)S(1)} %copy-done.11, bf16[32,512]{1,0:T(8,128)(2,1)S(1)} %copy-done.6, bf16[8,256,256]{2,1,0:T(8,128)(2,1)S(1)} %copy-done.1), custom_call_target="tpu_custom_call" | custom-call | flops 33554432 | bytes 1200000 | tf_op jit(solution)/shard_map/near/pallas_call | solution.py:157
  14.8 5.0 %all-to-all-done.got_ref = bf16[32,48,128]{2,1,0:T(8,128)(2,1)S(1)} async-done(((bf16[32,48,128]{2,1,0:T(8,128)(2,1)}), bf16[32,48,128]{2,1,0:T(8,128)(2,1)S(1)}, u32[]{:S(2)}, u32[]{:S(2)}) %all-to-all-start) | async-done | bytes 393248 | tf_op jit(solution)/shard_map/all_to_all | solution.py:142
  19.8 0.0 copy-start.5
  19.8 1.0 %copy-done.5 = bf16[24,64,128]{2,1,0:T(8,128)(2,1)S(1)} copy-done((bf16[24,64,128]{2,1,0:T(8,128)(2,1)S(1)}, bf16[24,64,128]{2,1,0:T(8,128)(2,1)}, u32[]{:S(2)}) %copy-start.5) | copy-done | bytes 393240
  20.8 1.8 %trees.1 = bf16[16,32,128]{2,1,0:T(8,128)(2,1)S(1)} custom-call(s32[8,128]{1,0:T(8,128)S(1)} %get-tuple-element.11.lists_in, bf16[32,48,128]{2,1,0:T(8,128)(2,1)S(1)} %all-to-all-done.got_ref, bf16[24,64,128]{2,1,0:T(8,128)(2,1)S(1)} %copy-done.5, bf16[64,64,128]{2,1,0:T(8,128)(2,1)S(1)} %get-tuple-element.14.coupling_ref, ...), custom_call_target="tpu_custom_call" | custom-call | tf_op jit(solution)/shard_map/trees/pallas_call | solution.py:167
  22.6 0.0 copy-start.7
  22.6 29.1 %all_to_all.10.got_ref = bf16[16,32,128]{2,1,0:T(8,128)(2,1)S(1)} all-to-all(bf16[16,32,128]{2,1,0:T(8,128)(2,1)S(1)} %trees.1), channel_id=1, replica_groups=mesh['row'=32,'col'=16] {'col'}, dimensions={0} | all-to-all | bytes 262144 | tf_op jit(solution)/shard_map/all_to_all | solution.py:178
  51.7 0.0 copy-done.7
  51.7 0.8 %outputs.1 = bf16[32,512]{1,0:T(8,128)(2,1)} custom-call(bf16[16,32,128]{2,1,0:T(8,128)(2,1)S(1)} %all_to_all.10.got_ref, bf16[2,64,256]{2,1,0:T(8,128)(2,1)S(1)} %copy-done.7, f32[2,32,256]{2,1,0:T(8,128)S(1)} %near.1.near_ref), custom_call_target="tpu_custom_call" | custom-call | tf_op jit(solution)/shard_map/outputs/pallas_call | solution.py:179
Async XLA Ops:
  0.0 9.5 %copy-start = (bf16[128,4096]{1,0:T(8,128)(2,1)S(1)}, bf16[128,4096]{1,0:T(8,128)(2,1)}, u32[]{:S(2)}) copy-start(bf16[128,4096]{1,0:T(8,128)(2,1)} %coupling_ref.1) | copy-start | bytes 3145732
  2.0 7.5 %copy-start.8 = (s32[4,32]{1,0:T(4,128)S(1)}, s32[4,32]{1,0:T(4,128)}, u32[]{:S(2)}) copy-start(s32[4,32]{1,0:T(4,128)} %rows_ref.2) | copy-start | bytes 1540
  2.0 7.5 %copy-start.9 = (s32[4,32]{1,0:T(4,128)S(1)}, s32[4,32]{1,0:T(4,128)}, u32[]{:S(2)}) copy-start(s32[4,32]{1,0:T(4,128)} %cols_ref.2) | copy-start | bytes 1540
  2.0 17.8 %all-to-all-start = ((bf16[32,48,128]{2,1,0:T(8,128)(2,1)}), bf16[32,48,128]{2,1,0:T(8,128)(2,1)S(1)}, u32[]{:S(2)}, u32[]{:S(2)}) async-start(bf16[32,48,128]{2,1,0:T(8,128)(2,1)} %moments.1), calls=%async_computation | async-start | bytes 786432 | tf_op jit(solution)/shard_map/all_to_all | solution.py:142
  9.5 1.0 %copy-start.2 = (bf16[1,56,4096]{2,1,0:T(8,128)(2,1)S(1)}, bf16[1,56,4096]{2,1,0:T(8,128)(2,1)}, u32[]{:S(2)}) copy-start(bf16[1,56,4096]{2,1,0:T(8,128)(2,1)} %links_ref.2) | copy-start | bytes 1376260
  10.5 1.0 %copy-start.3 = (bf16[1,48,4096]{2,1,0:T(8,128)(2,1)S(1)}, bf16[1,48,4096]{2,1,0:T(8,128)(2,1)}, u32[]{:S(2)}) copy-start(bf16[1,48,4096]{2,1,0:T(8,128)(2,1)} %top_ref.1) | copy-start | bytes 1179652
  11.5 2.4 %copy-start.1 = (bf16[8,256,256]{2,1,0:T(8,128)(2,1)S(1)}, bf16[8,256,256]{2,1,0:T(8,128)(2,1)}, u32[]{:S(2)}) copy-start(bf16[8,256,256]{2,1,0:T(8,128)(2,1)} %near_ref.1) | copy-start | bytes 3145732
  11.5 2.4 %copy-start.6 = (bf16[32,512]{1,0:T(8,128)(2,1)S(1)}, bf16[32,512]{1,0:T(8,128)(2,1)}, u32[]{:S(2)}) copy-start(bf16[32,512]{1,0:T(8,128)(2,1)} %x_ref.3) | copy-start | bytes 98308
  11.5 2.4 %copy-start.10 = (s32[8]{0:T(128)S(1)}, s32[8]{0:T(128)}, u32[]{:S(2)}) copy-start(s32[8]{0:T(128)} %rows_ref.3) | copy-start | bytes 100
  11.5 2.4 %copy-start.11 = (s32[8]{0:T(128)S(1)}, s32[8]{0:T(128)}, u32[]{:S(2)}) copy-start(s32[8]{0:T(128)} %cols_ref.3) | copy-start | bytes 100
  13.2 0.8 %copy-start.4 = (bf16[24,64,128]{2,1,0:T(8,128)(2,1)}, bf16[24,64,128]{2,1,0:T(8,128)(2,1)S(1)}, u32[]{:S(2)}) copy-start(bf16[24,64,128]{2,1,0:T(8,128)(2,1)S(1)} %get-tuple-element.13.top_ref) | copy-start | bytes 1179652
  19.8 1.0 %copy-start.5 = (bf16[24,64,128]{2,1,0:T(8,128)(2,1)S(1)}, bf16[24,64,128]{2,1,0:T(8,128)(2,1)}, u32[]{:S(2)}) copy-start(bf16[24,64,128]{2,1,0:T(8,128)(2,1)} %copy-done.4) | copy-start | bytes 1179652
  22.6 29.1 %copy-start.7 = (bf16[2,64,256]{2,1,0:T(8,128)(2,1)S(1)}, bf16[2,64,256]{2,1,0:T(8,128)(2,1)}, u32[]{:S(2)}) copy-start(bf16[2,64,256]{2,1,0:T(8,128)(2,1)} %basis_ref.3) | copy-start | bytes 196612

commit v4 on v3

--- a/solution.py
+++ b/solution.py
@@ -19,10 +19,6 @@
 
 def smem():
     return pl.BlockSpec(memory_space=pltpu.SMEM)
-
-
-def out_vmem(shape, dtype):
-    return pltpu.VMEM(shape, dtype)
 
 
 def moments_kernel(x_ref, basis_ref, links_ref, out_ref):
@@ -54,12 +50,27 @@
     return ref[place, :, 64 * side : 64 * (side + 1)]
 
 
-def unpack_kernel(coupling_ref, top_ref, links_ref, rows_ref, cols_ref, blocks_ref, up_ref, down_ref, lists_ref):
-    lists_ref[0:4, 0:32] = rows_ref[...]
-    lists_ref[4:8, 0:32] = cols_ref[...]
-    blocks_ref[...] = beside(coupling_ref[...].reshape(128, 64, 64))
-    up_ref[...] = beside(top_ref[0].reshape(48, 64, 64))
-    links = links_ref[0].reshape(56, 64, 64)
+def prepare_kernel(
+    coupling_in, top_in, links_in, rows_in, cols_in, near_in, x_in, near_rows_in, near_cols_in,
+    blocks_ref, up_ref, down_ref, rows_ref, cols_ref, nearby_ref,
+    coupling_ref, top_ref, links_ref, near_ref, x_ref, near_rows_ref, near_cols_ref, sems,
+):
+    pairs = (
+        (links_in.at[0], links_ref),
+        (top_in.at[0], top_ref),
+        (coupling_in, coupling_ref),
+        (near_rows_in, near_rows_ref),
+        (near_cols_in, near_cols_ref),
+        (x_in, x_ref),
+        (near_in, near_ref),
+        (rows_in, rows_ref),
+        (cols_in, cols_ref),
+    )
+    copies = [pltpu.make_async_copy(source, target, sems.at[i]) for i, (source, target) in enumerate(pairs)]
+    for copy in copies:
+        copy.start()
+    copies[0].wait()
+    links = links_ref[...].reshape(56, 64, 64)
     for b in range(16):
         one = jnp.concatenate([links[2 * b], links[2 * b + 1]], axis=1)
         two = dot(links[32 + b], one).astype(BF16)
@@ -67,15 +78,25 @@
         down_ref[b, 0:64, :] = one
         down_ref[b, 64:128, :] = two
         down_ref[b, 128:192, :] = three
+    copies[1].wait()
+    up_ref[...] = beside(top_ref[...].reshape(48, 64, 64))
+    copies[2].wait()
+    blocks_ref[...] = beside(coupling_ref[...].reshape(128, 64, 64))
+    for copy in copies[3:7]:
+        copy.wait()
+    nearby_ref[...] = jnp.zeros_like(nearby_ref)
+    for s in range(8):
+        start = pl.multiple_of(near_cols_ref[s] * 256, 256)
+        nearby_ref[near_rows_ref[s]] += dot(x_ref[:, pl.ds(start, 256)], near_ref[s])
+    for copy in copies[7:]:
+        copy.wait()
 
 
 def tree_kernel(
-    lists_in, got_ref, top_ref, coupling_ref, down_ref, out_ref,
-    mom0, mom1, mom2, mom3, acc0, acc1, acc2, acc3, lists_ref, sem,
+    rows_ref, cols_ref, got_ref, top_ref, coupling_ref, down_ref, out_ref,
+    mom0, mom1, mom2, mom3, acc0, acc1, acc2, acc3,
 ):
     mom, acc = (mom0, mom1, mom2, mom3), (acc0, acc1, acc2, acc3)
-    copy = pltpu.make_async_copy(lists_in, lists_ref, sem)
-    copy.start()
     for a in range(32):
         parent = got_ref[a, 32:48, :]
         mom1[a, 0:16] = parent[:, 0:64]
@@ -90,22 +111,14 @@
         mom3[p] = (dot(mom2[2 * p], matrix(top_ref, 32 + 2 * p)) + dot(mom2[2 * p + 1], matrix(top_ref, 33 + 2 * p))).astype(BF16)
     for depth in range(4):
         acc[depth][...] = jnp.zeros_like(acc[depth])
-    copy.wait()
     for s in range(32):
         for depth in range(4):
-            q, p = lists_ref[4 + depth, s], lists_ref[depth, s]
+            q, p = cols_ref[depth, s], rows_ref[depth, s]
             acc[depth][p] += dot(mom[depth][q], matrix(coupling_ref, depth * 32 + s))
     for b in range(16):
         upper = jnp.concatenate([acc1[b], acc2[b // 2], acc3[b // 4]], axis=1).astype(BF16)
         own = jnp.concatenate([acc0[2 * b], acc0[2 * b + 1]], axis=1)
         out_ref[b] = (own + dot(upper, down_ref[b])).astype(BF16)
-
-
-def near_kernel(rows_ref, cols_ref, x_ref, near_ref, out_ref):
-    out_ref[...] = jnp.zeros_like(out_ref)
-    for s in range(8):
-        start = pl.multiple_of(cols_ref[s] * 256, 256)
-        out_ref[rows_ref[s]] += dot(x_ref[:, pl.ds(start, 256)], near_ref[s])
 
 
 def output_kernel(got_ref, basis_ref, near_ref, out_ref):
@@ -140,41 +153,46 @@
         name="moments",
     )(columns_x, col_basis, col_links)
     gathered = lax.all_to_all(message, "row", 0, 0)
-    blocks, up, down, lists = pl.pallas_call(
-        unpack_kernel,
+    blocks, up, down, rows, cols, nearby = pl.pallas_call(
+        prepare_kernel,
         out_shape=[
-            out_vmem((64, 64, 128), BF16),
-            out_vmem((24, 64, 128), BF16),
-            out_vmem((16, 192, 128), BF16),
-            out_vmem((8, 128), jnp.int32),
+            pltpu.VMEM((64, 64, 128), BF16),
+            pltpu.VMEM((24, 64, 128), BF16),
+            pltpu.VMEM((16, 192, 128), BF16),
+            pltpu.SMEM((4, 32), jnp.int32),
+            pltpu.SMEM((4, 32), jnp.int32),
+            pltpu.VMEM((2, 32, 256), F32),
         ],
-        in_specs=[vmem()] * 5,
-        out_specs=[vmem()] * 4,
-        compiler_params=pltpu.CompilerParams(vmem_limit_bytes=16 * 1024 * 1024),
-        cost_estimate=pl.CostEstimate(flops=0, bytes_accessed=8_000_000, transcendentals=0),
-        name="unpack",
-    )(coupling, col_top_links, row_links, coupling_rows, coupling_cols)
-    nearby = pl.pallas_call(
-        near_kernel,
-        out_shape=out_vmem((2, 32, 256), F32),
-        in_specs=[smem()] * 2 + [vmem()] * 2,
-        out_specs=vmem(),
-        compiler_params=pltpu.CompilerParams(vmem_limit_bytes=16 * 1024 * 1024),
-        cost_estimate=pl.CostEstimate(flops=33_554_432, bytes_accessed=1_200_000, transcendentals=0),
-        name="near",
-    )(near_rows, near_cols, columns_x, near_blocks)
+        in_specs=[pl.BlockSpec(memory_space=pl.ANY)] * 9,
+        out_specs=[vmem()] * 3 + [smem()] * 2 + [vmem()],
+        scratch_shapes=[
+            pltpu.VMEM((128, 4096), BF16),
+            pltpu.VMEM((48, 4096), BF16),
+            pltpu.VMEM((56, 4096), BF16),
+            pltpu.VMEM((8, 256, 256), BF16),
+            pltpu.VMEM((32, 512), BF16),
+            pltpu.SMEM((8,), jnp.int32),
+            pltpu.SMEM((8,), jnp.int32),
+            pltpu.SemaphoreType.DMA((9,)),
+        ],
+        compiler_params=pltpu.CompilerParams(vmem_limit_bytes=60 * 1024 * 1024),
+        cost_estimate=pl.CostEstimate(flops=33_554_432, bytes_accessed=8_000_000, transcendentals=0),
+        name="prepare",
+    )(
+        coupling, col_top_links, row_links, coupling_rows, coupling_cols,
+        near_blocks, columns_x, near_rows, near_cols,
+    )
     gathered, nearby = lax.optimization_barrier((gathered, nearby))
     partials = pl.pallas_call(
         tree_kernel,
         out_shape=jax.ShapeDtypeStruct((16, 32, 128), BF16),
-        in_specs=[vmem()] * 5,
+        in_specs=[smem()] * 2 + [vmem()] * 4,
         out_specs=vmem(),
         scratch_shapes=[pltpu.VMEM((64 >> depth, 32, 64), BF16) for depth in range(4)]
-        + [pltpu.VMEM((32 >> depth, 32, 64), F32) for depth in range(4)]
-        + [pltpu.SMEM((8, 128), jnp.int32), pltpu.SemaphoreType.DMA],
+        + [pltpu.VMEM((32 >> depth, 32, 64), F32) for depth in range(4)],
         compiler_params=pltpu.CompilerParams(vmem_limit_bytes=16 * 1024 * 1024),
         name="trees",
-    )(lists, gathered, up, blocks, down)
+    )(rows, cols, gathered, up, blocks, down)
     scattered = lax.all_to_all(partials, "col", 0, 0)
     return pl.pallas_call(
         output_kernel,

time: 52.9 us -> 51.3 us (0.970)
  local copies, waits for them, and re-layouts: 3.79 us -> 0.01 us
  waiting for transfers between devices: 5 us -> 6.97 us
    unnamed x24 -> x2, local copies, waits for them, and re-layouts: 3.79 us -> 0.01 us
    all_to_all x1, waiting for transfers between devices: 5 us -> 6.97 us  [local(): gathered = lax.all_to_all(message, 'row', 0, 0)]
    pallas_call x2 -> x1, Pallas kernels: 2.46 us -> 3.32 us  [local(): pl.pallas_call(prepare_kernel, out_shape=[pltpu.VMEM((64, 64, 128), BF16)...]
  transfers between devices with their start and end apart: 1 -> 1, of which waited for: 1 -> 1; matrix products, arithmetic and copies ran while one was open for 0% -> 0% of each run, Pallas kernels for 5% -> 7%
where the time goes in v4:
time: 51.3 us; the launch traced here: 51 us
  blocking collectives  29.1 us (57%)
  Pallas kernels  7.59 us (15%)
  starting transfers between devices  7.32 us (14%)
  waiting for transfers between devices  6.97 us (14%)
    all_to_all x1, blocking collectives, local(): scattered = lax.all_to_all(partials, 'col', 0, 0)  29.1 us
    all_to_all x1, starting transfers between devices, local(): gathered = lax.all_to_all(message, 'row', 0, 0)  7.32 us
    all_to_all x1, waiting for transfers between devices, local(): gathered = lax.all_to_all(message, 'row', 0, 0)  6.97 us
    pallas_call x1, Pallas kernels, local(): pl.pallas_call(prepare_kernel, out_shape=[pltpu.VMEM((64, 64, 128), BF16)...  3.32 us
    pallas_call x1, Pallas kernels, local(): pl.pallas_call(moments_kernel, out_shape=jax.ShapeDtypeStruct((32, 48, 12...  1.92 us
    pallas_call x1, Pallas kernels, local(): pl.pallas_call(tree_kernel, out_shape=jax.ShapeDtypeStruct((16, 32, 128),...  1.52 us
  transfers between devices with their start and end apart: 1, of which 1 were waited for; matrix products, arithmetic and copies ran while one was open for 0% of the time, Pallas kernels for 7%

profile of v4, /device:TPU:32, one launch (start us, length us, event | category | flops | bytes accessed | tf_op | source)
XLA Modules:
  0.0 51.0 jit_solution(13552983348615597233)
XLA Ops:
  0.0 1.9 %moments.1 = bf16[32,48,128]{2,1,0:T(8,128)(2,1)} custom-call(bf16[32,512]{1,0:T(8,128)(2,1)} %x_ref.1, bf16[2,64,256]{2,1,0:T(8,128)(2,1)} %basis_ref.2, bf16[2,4096]{1,0:T(2,128)(2,1)} %links_ref.1), custom_call_target="tpu_custom_call" | custom-call | tf_op jit(solution)/shard_map/moments/pallas_call | solution.py:148
  1.9 7.3 %all-to-all-start = ((bf16[32,48,128]{2,1,0:T(8,128)(2,1)}), bf16[32,48,128]{2,1,0:T(8,128)(2,1)S(1)}, u32[]{:S(2)}, u32[]{:S(2)}) async-start(bf16[32,48,128]{2,1,0:T(8,128)(2,1)} %moments.1), calls=%async_computation | async-start | bytes 786432 | tf_op jit(solution)/shard_map/all_to_all | solution.py:155
  9.3 3.3 %prepare.1 = (bf16[64,64,128]{2,1,0:T(8,128)(2,1)S(1)}, bf16[24,64,128]{2,1,0:T(8,128)(2,1)S(1)}, bf16[16,192,128]{2,1,0:T(8,128)(2,1)S(1)}, s32[4,32]{1,0:T(4,1...) custom-call(bf16[128,4096]{1,0:T(8,128)(2,1)} %coupling_in.1, bf16[1,48,4096]{2,1,0:T(8,128)(2,1)} %top_in.1, ...), custom_call_target="tpu_custom_call" | custom-call | flops 33554432 | bytes 8000000 | tf_op jit(solution)/shard_map/prepare/pallas_call | solution.py:156
  12.6 7.0 %all-to-all-done.got_ref = bf16[32,48,128]{2,1,0:T(8,128)(2,1)S(1)} async-done(((bf16[32,48,128]{2,1,0:T(8,128)(2,1)}), bf16[32,48,128]{2,1,0:T(8,128)(2,1)S(1)}, u32[]{:S(2)}, u32[]{:S(2)}) %all-to-all-start) | async-done | bytes 393248 | tf_op jit(solution)/shard_map/all_to_all | solution.py:155
  19.6 1.5 %trees.1 = bf16[16,32,128]{2,1,0:T(8,128)(2,1)S(1)} custom-call(s32[4,32]{1,0:T(4,128)S(4)} %get-tuple-element.13.rows_ref, s32[4,32]{1,0:T(4,128)S(4)} %get-tuple-element.14.cols_ref, bf16[32,48,128]{2,1,0:T(8,128)(2,1)S(1)} %all-to-all-done.got_ref, bf16[24,64,128]{2,1,0:T(8,128)(2,1)S(1)} %get-tuple-element.17.top_ref, ...), custom_call_target="tpu_custom_call" | custom-call | tf_op jit(solution)/shard_map/trees/pallas_call | solution.py:186
  21.1 0.0 copy-start
  21.1 29.1 %all_to_all.10.got_ref = bf16[16,32,128]{2,1,0:T(8,128)(2,1)S(1)} all-to-all(bf16[16,32,128]{2,1,0:T(8,128)(2,1)S(1)} %trees.1), channel_id=1, replica_groups=mesh['row'=32,'col'=16] {'col'}, dimensions={0} | all-to-all | bytes 262144 | tf_op jit(solution)/shard_map/all_to_all | solution.py:196
  50.2 0.0 copy-done
  50.2 0.8 %outputs.1 = bf16[32,512]{1,0:T(8,128)(2,1)} custom-call(bf16[16,32,128]{2,1,0:T(8,128)(2,1)S(1)} %all_to_all.10.got_ref, bf16[2,64,256]{2,1,0:T(8,128)(2,1)S(1)} %copy-done, f32[2,32,256]{2,1,0:T(8,128)S(1)} %get-tuple-element.20.near_ref), custom_call_target="tpu_custom_call" | custom-call | tf_op jit(solution)/shard_map/outputs/pallas_call | solution.py:197
Async XLA Ops:
  1.9 17.6 %all-to-all-start = ((bf16[32,48,128]{2,1,0:T(8,128)(2,1)}), bf16[32,48,128]{2,1,0:T(8,128)(2,1)S(1)}, u32[]{:S(2)}, u32[]{:S(2)}) async-start(bf16[32,48,128]{2,1,0:T(8,128)(2,1)} %moments.1), calls=%async_computation | async-start | bytes 786432 | tf_op jit(solution)/shard_map/all_to_all | solution.py:155
  21.1 29.1 %copy-start = (bf16[2,64,256]{2,1,0:T(8,128)(2,1)S(1)}, bf16[2,64,256]{2,1,0:T(8,128)(2,1)}, u32[]{:S(2)}) copy-start(bf16[2,64,256]{2,1,0:T(8,128)(2,1)} %basis_ref.3) | copy-start | bytes 196612

commit v5 on v4

--- a/solution.py
+++ b/solution.py
@@ -4,6 +4,9 @@
 from jax.experimental import pallas as pl
 from jax.experimental.pallas import tpu as pltpu
 from jax.sharding import PartitionSpec as P
+
+ROW_ORDER = [(20 + j) % 32 for j in range(32)]
+COL_ORDER = [(8 + j) % 16 for j in range(16)]
 
 F32 = jnp.float32
 BF16 = jnp.bfloat16
@@ -97,14 +100,14 @@
     mom0, mom1, mom2, mom3, acc0, acc1, acc2, acc3,
 ):
     mom, acc = (mom0, mom1, mom2, mom3), (acc0, acc1, acc2, acc3)
-    for a in range(32):
-        parent = got_ref[a, 32:48, :]
+    for j, a in enumerate(ROW_ORDER):
+        parent = got_ref[j, 32:48, :]
         mom1[a, 0:16] = parent[:, 0:64]
         mom1[a, 16:32] = parent[:, 64:128]
     for p in range(16):
         mom2[p] = (dot(mom1[2 * p], matrix(top_ref, 2 * p)) + dot(mom1[2 * p + 1], matrix(top_ref, 2 * p + 1))).astype(BF16)
-    for a in range(32):
-        both = got_ref[a, 0:32, :]
+    for j, a in enumerate(ROW_ORDER):
+        both = got_ref[j, 0:32, :]
         mom0[2 * a] = both[:, 0:64]
         mom0[2 * a + 1] = both[:, 64:128]
     for p in range(8):
@@ -115,10 +118,10 @@
         for depth in range(4):
             q, p = cols_ref[depth, s], rows_ref[depth, s]
             acc[depth][p] += dot(mom[depth][q], matrix(coupling_ref, depth * 32 + s))
-    for b in range(16):
+    for j, b in enumerate(COL_ORDER):
         upper = jnp.concatenate([acc1[b], acc2[b // 2], acc3[b // 4]], axis=1).astype(BF16)
         own = jnp.concatenate([acc0[2 * b], acc0[2 * b + 1]], axis=1)
-        out_ref[b] = (own + dot(upper, down_ref[b])).astype(BF16)
+        out_ref[j] = (own + dot(upper, down_ref[b])).astype(BF16)
 
 
 def output_kernel(got_ref, basis_ref, near_ref, out_ref):
@@ -152,7 +155,7 @@
         out_specs=vmem(),
         name="moments",
     )(columns_x, col_basis, col_links)
-    gathered = lax.all_to_all(message, "row", 0, 0)
+    gathered = lax.all_to_all(message, "row", 0, 0, axis_index_groups=[ROW_ORDER])
     blocks, up, down, rows, cols, nearby = pl.pallas_call(
         prepare_kernel,
         out_shape=[
@@ -193,7 +196,7 @@
         compiler_params=pltpu.CompilerParams(vmem_limit_bytes=16 * 1024 * 1024),
         name="trees",
     )(rows, cols, gathered, up, blocks, down)
-    scattered = lax.all_to_all(partials, "col", 0, 0)
+    scattered = lax.all_to_all(partials, "col", 0, 0, axis_index_groups=[COL_ORDER])
     return pl.pallas_call(
         output_kernel,
         out_shape=jax.ShapeDtypeStruct((32, 512), BF16),

time: 51.3 us -> 45.6 us (0.89)
  the two profiles are of different devices: /device:TPU:32 before, /device:TPU:1 now
where the time goes in v5:
time: 45.6 us; the launch traced here: 45.2 us
  blocking collectives  21.5 us (47%)
  starting transfers between devices  13.9 us (30%)
  Pallas kernels  7.59 us (17%)
  waiting for transfers between devices  2.23 us (5%)
    all_to_all x1, blocking collectives, local(): lax.all_to_all(partials, 'col', 0, 0, axis_index_groups=[COL_ORDER])  21.5 us
    all_to_all x1, starting transfers between devices, local(): lax.all_to_all(message, 'row', 0, 0, axis_index_groups=[ROW_ORDER])  13.9 us
    pallas_call x1, Pallas kernels, local(): pl.pallas_call(prepare_kernel, out_shape=[pltpu.VMEM((64, 64, 128), BF16)...  3.32 us
    all_to_all x1, waiting for transfers between devices, local(): lax.all_to_all(message, 'row', 0, 0, axis_index_groups=[ROW_ORDER])  2.23 us
    pallas_call x1, Pallas kernels, local(): pl.pallas_call(moments_kernel, out_shape=jax.ShapeDtypeStruct((32, 48, 12...  1.92 us
    pallas_call x1, Pallas kernels, local(): pl.pallas_call(tree_kernel, out_shape=jax.ShapeDtypeStruct((16, 32, 128),...  1.52 us
  transfers between devices with their start and end apart: 1, of which 1 were waited for; matrix products, arithmetic and copies ran while one was open for 0% of the time, Pallas kernels for 7%

profile of v5, /device:TPU:1, one launch (start us, length us, event | category | flops | bytes accessed | tf_op | source)
XLA Modules:
  0.0 45.2 jit_solution(10737748784238300901)
XLA Ops:
  0.0 1.9 %moments.1 = bf16[32,48,128]{2,1,0:T(8,128)(2,1)} custom-call(bf16[32,512]{1,0:T(8,128)(2,1)} %x_ref.1, bf16[2,64,256]{2,1,0:T(8,128)(2,1)} %basis_ref.2, bf16[2,4096]{1,0:T(2,128)(2,1)} %links_ref.1), custom_call_target="tpu_custom_call" | custom-call | tf_op jit(solution)/shard_map/moments/pallas_call | solution.py:151
  1.9 13.9 %all-to-all-start = ((bf16[32,48,128]{2,1,0:T(8,128)(2,1)}), bf16[32,48,128]{2,1,0:T(8,128)(2,1)S(1)}, u32[]{:S(2)}, u32[]{:S(2)}) async-start(bf16[32,48,128]{2,1,0:T(8,128)(2,1)} %moments.1), calls=%async_computation | async-start | bytes 786432 | tf_op jit(solution)/shard_map/all_to_all | solution.py:158
  15.8 3.3 %prepare.1 = (bf16[64,64,128]{2,1,0:T(8,128)(2,1)S(1)}, bf16[24,64,128]{2,1,0:T(8,128)(2,1)S(1)}, bf16[16,192,128]{2,1,0:T(8,128)(2,1)S(1)}, s32[4,32]{1,0:T(4,1...) custom-call(bf16[128,4096]{1,0:T(8,128)(2,1)} %coupling_in.1, bf16[1,48,4096]{2,1,0:T(8,128)(2,1)} %top_in.1, ...), custom_call_target="tpu_custom_call" | custom-call | flops 33554432 | bytes 8000000 | tf_op jit(solution)/shard_map/prepare/pallas_call | solution.py:159
  19.1 2.2 %all-to-all-done.got_ref = bf16[32,48,128]{2,1,0:T(8,128)(2,1)S(1)} async-done(((bf16[32,48,128]{2,1,0:T(8,128)(2,1)}), bf16[32,48,128]{2,1,0:T(8,128)(2,1)S(1)}, u32[]{:S(2)}, u32[]{:S(2)}) %all-to-all-start) | async-done | bytes 393248 | tf_op jit(solution)/shard_map/all_to_all | solution.py:158
  21.4 1.5 %trees.1 = bf16[16,32,128]{2,1,0:T(8,128)(2,1)S(1)} custom-call(s32[4,32]{1,0:T(4,128)S(4)} %get-tuple-element.13.rows_ref, s32[4,32]{1,0:T(4,128)S(4)} %get-tuple-element.14.cols_ref, bf16[32,48,128]{2,1,0:T(8,128)(2,1)S(1)} %all-to-all-done.got_ref, bf16[24,64,128]{2,1,0:T(8,128)(2,1)S(1)} %get-tuple-element.17.top_ref, ...), custom_call_target="tpu_custom_call" | custom-call | tf_op jit(solution)/shard_map/trees/pallas_call | solution.py:189
  22.9 0.0 copy-start
  22.9 21.5 %all_to_all.10.got_ref = bf16[16,32,128]{2,1,0:T(8,128)(2,1)S(1)} all-to-all(bf16[16,32,128]{2,1,0:T(8,128)(2,1)S(1)} %trees.1), channel_id=1, replica_groups={{8,9,10,11,12,13,14,15,0,1,2,3,4,5,6,7},{24,25,26,27,28,29,30,31,16,17,..., dimensions={0} | all-to-all | bytes 262144 | tf_op jit(solution)/shard_map/all_to_all | solution.py:199
  44.4 0.0 copy-done
  44.4 0.8 %outputs.1 = bf16[32,512]{1,0:T(8,128)(2,1)} custom-call(bf16[16,32,128]{2,1,0:T(8,128)(2,1)S(1)} %all_to_all.10.got_ref, bf16[2,64,256]{2,1,0:T(8,128)(2,1)S(1)} %copy-done, f32[2,32,256]{2,1,0:T(8,128)S(1)} %get-tuple-element.20.near_ref), custom_call_target="tpu_custom_call" | custom-call | tf_op jit(solution)/shard_map/outputs/pallas_call | solution.py:200
Async XLA Ops:
  1.9 19.5 %all-to-all-start = ((bf16[32,48,128]{2,1,0:T(8,128)(2,1)}), bf16[32,48,128]{2,1,0:T(8,128)(2,1)S(1)}, u32[]{:S(2)}, u32[]{:S(2)}) async-start(bf16[32,48,128]{2,1,0:T(8,128)(2,1)} %moments.1), calls=%async_computation | async-start | bytes 786432 | tf_op jit(solution)/shard_map/all_to_all | solution.py:158
  22.9 21.5 %copy-start = (bf16[2,64,256]{2,1,0:T(8,128)(2,1)S(1)}, bf16[2,64,256]{2,1,0:T(8,128)(2,1)}, u32[]{:S(2)}) copy-start(bf16[2,64,256]{2,1,0:T(8,128)(2,1)} %basis_ref.3) | copy-start | bytes 196612

commit v6 on v5

--- a/solution.py
+++ b/solution.py
@@ -5,7 +5,7 @@
 from jax.experimental.pallas import tpu as pltpu
 from jax.sharding import PartitionSpec as P
 
-ROW_ORDER = [(20 + j) % 32 for j in range(32)]
+CHIP_ORDER = [(10 + j) % 16 for j in range(16)]
 COL_ORDER = [(8 + j) % 16 for j in range(16)]
 
 F32 = jnp.float32
@@ -100,14 +100,15 @@
     mom0, mom1, mom2, mom3, acc0, acc1, acc2, acc3,
 ):
     mom, acc = (mom0, mom1, mom2, mom3), (acc0, acc1, acc2, acc3)
-    for j, a in enumerate(ROW_ORDER):
-        parent = got_ref[j, 32:48, :]
+    received = [(2 * chip + core, core, j) for j, chip in enumerate(CHIP_ORDER) for core in range(2)]
+    for a, core, j in received:
+        parent = got_ref[core, j, 32:48, :]
         mom1[a, 0:16] = parent[:, 0:64]
         mom1[a, 16:32] = parent[:, 64:128]
     for p in range(16):
         mom2[p] = (dot(mom1[2 * p], matrix(top_ref, 2 * p)) + dot(mom1[2 * p + 1], matrix(top_ref, 2 * p + 1))).astype(BF16)
-    for j, a in enumerate(ROW_ORDER):
-        both = got_ref[j, 0:32, :]
+    for a, core, j in received:
+        both = got_ref[core, j, 0:32, :]
         mom0[2 * a] = both[:, 0:64]
         mom0[2 * a + 1] = both[:, 64:128]
     for p in range(8):
@@ -115,11 +116,14 @@
     for depth in range(4):
         acc[depth][...] = jnp.zeros_like(acc[depth])
     for s in range(32):
-        for depth in range(4):
-            q, p = cols_ref[depth, s], rows_ref[depth, s]
-            acc[depth][p] += dot(mom[depth][q], matrix(coupling_ref, depth * 32 + s))
+        for depth in (0, 1):
+            first, second = cols_ref[depth, s], cols_ref[depth + 2, s]
+            picked = jnp.concatenate([mom[depth][first], mom[depth + 2][second]], axis=0)
+            term = dot(picked, coupling_ref[depth * 32 + s])
+            acc[depth][rows_ref[depth, s]] += term[0:32, 0:64]
+            acc[depth + 2][rows_ref[depth + 2, s], :, 64:128] += term[32:64, 64:128]
     for j, b in enumerate(COL_ORDER):
-        upper = jnp.concatenate([acc1[b], acc2[b // 2], acc3[b // 4]], axis=1).astype(BF16)
+        upper = jnp.concatenate([acc1[b], acc2[b // 2, :, 64:128], acc3[b // 4, :, 64:128]], axis=1).astype(BF16)
         own = jnp.concatenate([acc0[2 * b], acc0[2 * b + 1]], axis=1)
         out_ref[j] = (own + dot(upper, down_ref[b])).astype(BF16)
 
@@ -150,12 +154,14 @@
 ):
     message = pl.pallas_call(
         moments_kernel,
-        out_shape=jax.ShapeDtypeStruct((32, 48, 128), BF16),
+        out_shape=jax.ShapeDtypeStruct((16, 48, 128), BF16),
         in_specs=[vmem()] * 3,
         out_specs=vmem(),
         name="moments",
     )(columns_x, col_basis, col_links)
-    gathered = lax.all_to_all(message, "row", 0, 0, axis_index_groups=[ROW_ORDER])
+    same_core = [[2 * chip + core for chip in CHIP_ORDER] for core in range(2)]
+    same_chip = [[2 * chip, 2 * chip + 1] for chip in range(16)]
+    arrived = lax.all_to_all(message, "row", 0, 0, axis_index_groups=same_core)
     blocks, up, down, rows, cols, nearby = pl.pallas_call(
         prepare_kernel,
         out_shape=[
@@ -185,14 +191,15 @@
         coupling, col_top_links, row_links, coupling_rows, coupling_cols,
         near_blocks, columns_x, near_rows, near_cols,
     )
-    gathered, nearby = lax.optimization_barrier((gathered, nearby))
+    arrived, nearby = lax.optimization_barrier((arrived, nearby))
+    gathered = lax.all_gather(arrived, "row", axis=0, axis_index_groups=same_chip)
     partials = pl.pallas_call(
         tree_kernel,
         out_shape=jax.ShapeDtypeStruct((16, 32, 128), BF16),
         in_specs=[smem()] * 2 + [vmem()] * 4,
         out_specs=vmem(),
         scratch_shapes=[pltpu.VMEM((64 >> depth, 32, 64), BF16) for depth in range(4)]
-        + [pltpu.VMEM((32 >> depth, 32, 64), F32) for depth in range(4)],
+        + [pltpu.VMEM((32 >> depth, 32, 64 if depth < 2 else 128), F32) for depth in range(4)],
         compiler_params=pltpu.CompilerParams(vmem_limit_bytes=16 * 1024 * 1024),
         name="trees",
     )(rows, cols, gathered, up, blocks, down)

time: 45.6 us -> 44.9 us (0.985)
  blocking collectives: 21.5 us -> 27.7 us
  starting transfers between devices: 13.9 us -> 9.55 us
  waiting for transfers between devices: 2.23 us -> 0.01 us
    all_gather x0 -> x1, blocking collectives: none -> 6.28 us  [local(): lax.all_gather(arrived, 'row', axis=0, axis_index_groups=same_chip)]
    all_to_all x1, starting transfers between devices: 13.9 us -> 9.55 us  [local(): arrived = lax.all_to_all(message, 'row', 0, 0, axis_index_groups=same_core)]
    all_to_all x1, waiting for transfers between devices: 2.23 us -> 0.01 us  [local(): arrived = lax.all_to_all(message, 'row', 0, 0, axis_index_groups=same_core)]
  transfers between devices with their start and end apart: 1 -> 1, of which waited for: 1 -> 0; matrix products, arithmetic and copies ran while one was open for 0% -> 0% of each run, Pallas kernels for 7% -> 7%
where the time goes in v6:
time: 44.9 us; the launch traced here: 44.6 us
  blocking collectives  27.7 us (62%)
  starting transfers between devices  9.55 us (21%)
  Pallas kernels  7.3 us (16%)
    all_to_all x1, blocking collectives, local(): lax.all_to_all(partials, 'col', 0, 0, axis_index_groups=[COL_ORDER])  21.4 us
    all_to_all x1, starting transfers between devices, local(): arrived = lax.all_to_all(message, 'row', 0, 0, axis_index_groups=same_core)  9.55 us
    all_gather x1, blocking collectives, local(): lax.all_gather(arrived, 'row', axis=0, axis_index_groups=same_chip)  6.28 us
    pallas_call x1, Pallas kernels, local(): pl.pallas_call(prepare_kernel, out_shape=[pltpu.VMEM((64, 64, 128), BF16)...  3.31 us
    pallas_call x1, Pallas kernels, local(): pl.pallas_call(moments_kernel, out_shape=jax.ShapeDtypeStruct((16, 48, 12...  1.84 us
    pallas_call x1, Pallas kernels, local(): pl.pallas_call(tree_kernel, out_shape=jax.ShapeDtypeStruct((16, 32, 128),...  1.33 us
  transfers between devices with their start and end apart: 1, of which 0 were waited for; matrix products, arithmetic and copies ran while one was open for 0% of the time, Pallas kernels for 7%

profile of v6, /device:TPU:1, one launch (start us, length us, event | category | flops | bytes accessed | tf_op | source)
XLA Modules:
  0.0 44.6 jit_solution(8017852188190221743)
XLA Ops:
  0.0 1.8 %moments.1 = bf16[16,48,128]{2,1,0:T(8,128)(2,1)} custom-call(bf16[32,512]{1,0:T(8,128)(2,1)} %x_ref.1, bf16[2,64,256]{2,1,0:T(8,128)(2,1)} %basis_ref.2, bf16[2,4096]{1,0:T(2,128)(2,1)} %links_ref.1), custom_call_target="tpu_custom_call" | custom-call | tf_op jit(solution)/shard_map/moments/pallas_call | solution.py:155
  1.8 9.5 %all-to-all-start = ((bf16[16,48,128]{2,1,0:T(8,128)(2,1)}), bf16[16,48,128]{2,1,0:T(8,128)(2,1)S(1)}, u32[]{:S(2)}, u32[]{:S(2)}) async-start(bf16[16,48,128]{2,1,0:T(8,128)(2,1)} %moments.1), calls=%async_computation | async-start | bytes 393216 | tf_op jit(solution)/shard_map/all_to_all | solution.py:164
  11.4 3.3 %prepare.1 = (bf16[64,64,128]{2,1,0:T(8,128)(2,1)S(1)}, bf16[24,64,128]{2,1,0:T(8,128)(2,1)S(1)}, bf16[16,192,128]{2,1,0:T(8,128)(2,1)S(1)}, s32[4,32]{1,0:T(4,1...) custom-call(bf16[128,4096]{1,0:T(8,128)(2,1)} %coupling_in.1, bf16[1,48,4096]{2,1,0:T(8,128)(2,1)} %top_in.1, ...), custom_call_target="tpu_custom_call" | custom-call | flops 33554432 | bytes 8000000 | tf_op jit(solution)/shard_map/prepare/pallas_call | solution.py:165
  14.7 0.0 all-to-all-done
  14.7 6.3 %all-gather = bf16[32,48,128]{2,1,0:T(8,128)(2,1)S(1)} all-gather(bf16[16,48,128]{2,1,0:T(8,128)(2,1)S(1)} %all-to-all-done), channel_id=2, replica_groups={{0,16},{32,48},{64,80},{96,112},{128,144},{160,176},{192,208},{224,240}..., dimensions={0}, use_global_device_ids=true | all-gather | bytes 589824 | tf_op jit(solution)/shard_map/all_gather | solution.py:195
  21.0 1.3 %trees.1 = bf16[16,32,128]{2,1,0:T(8,128)(2,1)S(1)} custom-call(s32[4,32]{1,0:T(4,128)S(4)} %get-tuple-element.13.rows_ref, s32[4,32]{1,0:T(4,128)S(4)} %get-tuple-element.14.cols_ref, bf16[2,16,48,128]{3,2,1,0:T(8,128)(2,1)S(1)} %bitcast.1, bf16[24,64,128]{2,1,0:T(8,128)(2,1)S(1)} %get-tuple-element.17.top_ref, ...), custom_call_target="tpu_custom_call" | custom-call | tf_op jit(solution)/shard_map/trees/pallas_call | solution.py:196
  22.3 0.0 copy-start
  22.3 21.4 %all_to_all.10.got_ref = bf16[16,32,128]{2,1,0:T(8,128)(2,1)S(1)} all-to-all(bf16[16,32,128]{2,1,0:T(8,128)(2,1)S(1)} %trees.1), channel_id=1, replica_groups={{8,9,10,11,12,13,14,15,0,1,2,3,4,5,6,7},{24,25,26,27,28,29,30,31,16,17,..., dimensions={0} | all-to-all | bytes 262144 | tf_op jit(solution)/shard_map/all_to_all | solution.py:206
  43.7 0.0 copy-done
  43.7 0.8 %outputs.1 = bf16[32,512]{1,0:T(8,128)(2,1)} custom-call(bf16[16,32,128]{2,1,0:T(8,128)(2,1)S(1)} %all_to_all.10.got_ref, bf16[2,64,256]{2,1,0:T(8,128)(2,1)S(1)} %copy-done, f32[2,32,256]{2,1,0:T(8,128)S(1)} %get-tuple-element.20.near_ref), custom_call_target="tpu_custom_call" | custom-call | tf_op jit(solution)/shard_map/outputs/pallas_call | solution.py:207
Async XLA Ops:
  1.8 12.9 %all-to-all-start = ((bf16[16,48,128]{2,1,0:T(8,128)(2,1)}), bf16[16,48,128]{2,1,0:T(8,128)(2,1)S(1)}, u32[]{:S(2)}, u32[]{:S(2)}) async-start(bf16[16,48,128]{2,1,0:T(8,128)(2,1)} %moments.1), calls=%async_computation | async-start | bytes 393216 | tf_op jit(solution)/shard_map/all_to_all | solution.py:164
  22.3 21.4 %copy-start = (bf16[2,64,256]{2,1,0:T(8,128)(2,1)S(1)}, bf16[2,64,256]{2,1,0:T(8,128)(2,1)}, u32[]{:S(2)}) copy-start(bf16[2,64,256]{2,1,0:T(8,128)(2,1)} %basis_ref.3) | copy-start | bytes 196612

commit v7 on v6

--- a/solution.py
+++ b/solution.py
@@ -6,7 +6,7 @@
 from jax.sharding import PartitionSpec as P
 
 CHIP_ORDER = [(10 + j) % 16 for j in range(16)]
-COL_ORDER = [(8 + j) % 16 for j in range(16)]
+COL_ORDER = [(8 + 7 * j) % 16 for j in range(16)]
 
 F32 = jnp.float32
 BF16 = jnp.bfloat16
@@ -46,6 +46,15 @@
 def beside(matrices):
     half = matrices.shape[0] // 2
     return jnp.concatenate([matrices[:half], matrices[half:]], axis=2)
+
+
+def paired(first, second):
+    columns = []
+    for i in range(0, first.shape[1], 128):
+        one, two = first[:, i : i + 128], second[:, i : i + 128]
+        columns.append(jnp.concatenate([one[:, 0:64], two[:, 0:64]], axis=1))
+        columns.append(jnp.concatenate([one[:, 64:128], two[:, 64:128]], axis=1))
+    return jnp.concatenate(columns, axis=1).reshape(first.shape[0], 64, 128)
 
 
 def matrix(ref, j):
@@ -84,7 +93,8 @@
     copies[1].wait()
     up_ref[...] = beside(top_ref[...].reshape(48, 64, 64))
     copies[2].wait()
-    blocks_ref[...] = beside(coupling_ref[...].reshape(128, 64, 64))
+    for i in range(0, 64, 16):
+        blocks_ref[i : i + 16] = paired(coupling_ref[i : i + 16], coupling_ref[64 + i : 80 + i])
     for copy in copies[3:7]:
         copy.wait()
     nearby_ref[...] = jnp.zeros_like(nearby_ref)

time: 44.9 us -> 44.9 us (level)
  transfers between devices with their start and end apart: 1 -> 1, of which waited for: 0 -> 0; matrix products, arithmetic and copies ran while one was open for 0% -> 0% of each run, Pallas kernels for 7% -> 6%
where the time goes in v7:
time: 44.9 us; the launch traced here: 44.6 us
  blocking collectives  28.1 us (63%)
  starting transfers between devices  9.55 us (21%)
  Pallas kernels  6.89 us (15%)
    all_to_all x1, blocking collectives, local(): lax.all_to_all(partials, 'col', 0, 0, axis_index_groups=[COL_ORDER])  21.4 us
    all_to_all x1, starting transfers between devices, local(): arrived = lax.all_to_all(message, 'row', 0, 0, axis_index_groups=same_core)  9.55 us
    all_gather x1, blocking collectives, local(): lax.all_gather(arrived, 'row', axis=0, axis_index_groups=same_chip)  6.71 us
    pallas_call x1, Pallas kernels, local(): pl.pallas_call(prepare_kernel, out_shape=[pltpu.VMEM((64, 64, 128), BF16)...  2.89 us
    pallas_call x1, Pallas kernels, local(): pl.pallas_call(moments_kernel, out_shape=jax.ShapeDtypeStruct((16, 48, 12...  1.84 us
    pallas_call x1, Pallas kernels, local(): pl.pallas_call(tree_kernel, out_shape=jax.ShapeDtypeStruct((16, 32, 128),...  1.33 us
  transfers between devices with their start and end apart: 1, of which 0 were waited for; matrix products, arithmetic and copies ran while one was open for 0% of the time, Pallas kernels for 6%

profile of v7, /device:TPU:1, one launch (start us, length us, event | category | flops | bytes accessed | tf_op | source)
XLA Modules:
  0.0 44.6 jit_solution(106485519432774690)
XLA Ops:
  0.0 1.8 %moments.1 = bf16[16,48,128]{2,1,0:T(8,128)(2,1)} custom-call(bf16[32,512]{1,0:T(8,128)(2,1)} %x_ref.1, bf16[2,64,256]{2,1,0:T(8,128)(2,1)} %basis_ref.2, bf16[2,4096]{1,0:T(2,128)(2,1)} %links_ref.1), custom_call_target="tpu_custom_call" | custom-call | tf_op jit(solution)/shard_map/moments/pallas_call | solution.py:165
  1.8 9.5 %all-to-all-start = ((bf16[16,48,128]{2,1,0:T(8,128)(2,1)}), bf16[16,48,128]{2,1,0:T(8,128)(2,1)S(1)}, u32[]{:S(2)}, u32[]{:S(2)}) async-start(bf16[16,48,128]{2,1,0:T(8,128)(2,1)} %moments.1), calls=%async_computation | async-start | bytes 393216 | tf_op jit(solution)/shard_map/all_to_all | solution.py:174
  11.4 2.9 %prepare.1 = (bf16[64,64,128]{2,1,0:T(8,128)(2,1)S(1)}, bf16[24,64,128]{2,1,0:T(8,128)(2,1)S(1)}, bf16[16,192,128]{2,1,0:T(8,128)(2,1)S(1)}, s32[4,32]{1,0:T(4,1...) custom-call(bf16[128,4096]{1,0:T(8,128)(2,1)} %coupling_in.1, bf16[1,48,4096]{2,1,0:T(8,128)(2,1)} %top_in.1, ...), custom_call_target="tpu_custom_call" | custom-call | flops 33554432 | bytes 8000000 | tf_op jit(solution)/shard_map/prepare/pallas_call | solution.py:175
  14.3 0.0 all-to-all-done
  14.3 6.7 %all-gather = bf16[32,48,128]{2,1,0:T(8,128)(2,1)S(1)} all-gather(bf16[16,48,128]{2,1,0:T(8,128)(2,1)S(1)} %all-to-all-done), channel_id=2, replica_groups={{0,16},{32,48},{64,80},{96,112},{128,144},{160,176},{192,208},{224,240}..., dimensions={0}, use_global_device_ids=true | all-gather | bytes 589824 | tf_op jit(solution)/shard_map/all_gather | solution.py:205
  21.0 1.3 %trees.1 = bf16[16,32,128]{2,1,0:T(8,128)(2,1)S(1)} custom-call(s32[4,32]{1,0:T(4,128)S(4)} %get-tuple-element.13.rows_ref, s32[4,32]{1,0:T(4,128)S(4)} %get-tuple-element.14.cols_ref, bf16[2,16,48,128]{3,2,1,0:T(8,128)(2,1)S(1)} %bitcast.1, bf16[24,64,128]{2,1,0:T(8,128)(2,1)S(1)} %get-tuple-element.17.top_ref, ...), custom_call_target="tpu_custom_call" | custom-call | tf_op jit(solution)/shard_map/trees/pallas_call | solution.py:206
  22.3 0.0 copy-start
  22.3 21.4 %all_to_all.10.got_ref = bf16[16,32,128]{2,1,0:T(8,128)(2,1)S(1)} all-to-all(bf16[16,32,128]{2,1,0:T(8,128)(2,1)S(1)} %trees.1), channel_id=1, replica_groups={{8,15,6,13,4,11,2,9,0,7,14,5,12,3,10,1},{24,31,22,29,20,27,18,25,16,23,..., dimensions={0} | all-to-all | bytes 262144 | tf_op jit(solution)/shard_map/all_to_all | solution.py:216
  43.8 0.0 copy-done
  43.8 0.8 %outputs.1 = bf16[32,512]{1,0:T(8,128)(2,1)} custom-call(bf16[16,32,128]{2,1,0:T(8,128)(2,1)S(1)} %all_to_all.10.got_ref, bf16[2,64,256]{2,1,0:T(8,128)(2,1)S(1)} %copy-done, f32[2,32,256]{2,1,0:T(8,128)S(1)} %get-tuple-element.20.near_ref), custom_call_target="tpu_custom_call" | custom-call | tf_op jit(solution)/shard_map/outputs/pallas_call | solution.py:217
Async XLA Ops:
  1.8 12.4 %all-to-all-start = ((bf16[16,48,128]{2,1,0:T(8,128)(2,1)}), bf16[16,48,128]{2,1,0:T(8,128)(2,1)S(1)}, u32[]{:S(2)}, u32[]{:S(2)}) async-start(bf16[16,48,128]{2,1,0:T(8,128)(2,1)} %moments.1), calls=%async_computation | async-start | bytes 393216 | tf_op jit(solution)/shard_map/all_to_all | solution.py:174
  22.3 21.4 %copy-start = (bf16[2,64,256]{2,1,0:T(8,128)(2,1)S(1)}, bf16[2,64,256]{2,1,0:T(8,128)(2,1)}, u32[]{:S(2)}) copy-start(bf16[2,64,256]{2,1,0:T(8,128)(2,1)} %basis_ref.3) | copy-start | bytes 196612

commit v8 on v7

--- a/solution.py
+++ b/solution.py
@@ -6,7 +6,7 @@
 from jax.sharding import PartitionSpec as P
 
 CHIP_ORDER = [(10 + j) % 16 for j in range(16)]
-COL_ORDER = [(8 + 7 * j) % 16 for j in range(16)]
+COL_ORDER = [(11 + j) % 16 for j in range(16)]
 
 F32 = jnp.float32
 BF16 = jnp.bfloat16
@@ -43,11 +43,6 @@
         out_ref[r, 32:48, :] = high
 
 
-def beside(matrices):
-    half = matrices.shape[0] // 2
-    return jnp.concatenate([matrices[:half], matrices[half:]], axis=2)
-
-
 def paired(first, second):
     columns = []
     for i in range(0, first.shape[1], 128):
@@ -55,11 +50,6 @@
         columns.append(jnp.concatenate([one[:, 0:64], two[:, 0:64]], axis=1))
         columns.append(jnp.concatenate([one[:, 64:128], two[:, 64:128]], axis=1))
     return jnp.concatenate(columns, axis=1).reshape(first.shape[0], 64, 128)
-
-
-def matrix(ref, j):
-    side, place = divmod(j, ref.shape[0])
-    return ref[place, :, 64 * side : 64 * (side + 1)]
 
 
 def prepare_kernel(
@@ -87,14 +77,17 @@
         one = jnp.concatenate([links[2 * b], links[2 * b + 1]], axis=1)
         two = dot(links[32 + b], one).astype(BF16)
         three = dot(links[48 + b // 2], two).astype(BF16)
-        down_ref[b, 0:64, :] = one
-        down_ref[b, 64:128, :] = two
-        down_ref[b, 128:192, :] = three
+        down_ref[b, 0:64, :] = two
+        down_ref[b, 64:128, :] = one
+        down_ref[b, 128:192, :] = jnp.zeros_like(one)
+        down_ref[b, 192:256, :] = three
     copies[1].wait()
-    up_ref[...] = beside(top_ref[...].reshape(48, 64, 64))
+    top = top_ref[...].reshape(48, 64, 64)
+    for p in range(24):
+        up_ref[p] = jnp.concatenate([top[2 * p], top[2 * p + 1]], axis=1)
     copies[2].wait()
-    for i in range(0, 64, 16):
-        blocks_ref[i : i + 16] = paired(coupling_ref[i : i + 16], coupling_ref[64 + i : 80 + i])
+    for place, i in ((0, 0), (16, 16), (32, 64), (48, 80)):
+        blocks_ref[place : place + 16] = paired(coupling_ref[i : i + 16], coupling_ref[i + 32 : i + 48])
     for copy in copies[3:7]:
         copy.wait()
     nearby_ref[...] = jnp.zeros_like(nearby_ref)
@@ -110,30 +103,33 @@
     mom0, mom1, mom2, mom3, acc0, acc1, acc2, acc3,
 ):
     mom, acc = (mom0, mom1, mom2, mom3), (acc0, acc1, acc2, acc3)
+    for depth in range(4):
+        acc[depth][...] = jnp.zeros_like(acc[depth])
     received = [(2 * chip + core, core, j) for j, chip in enumerate(CHIP_ORDER) for core in range(2)]
     for a, core, j in received:
         parent = got_ref[core, j, 32:48, :]
         mom1[a, 0:16] = parent[:, 0:64]
         mom1[a, 16:32] = parent[:, 64:128]
     for p in range(16):
-        mom2[p] = (dot(mom1[2 * p], matrix(top_ref, 2 * p)) + dot(mom1[2 * p + 1], matrix(top_ref, 2 * p + 1))).astype(BF16)
+        both = dot(mom1[2 * p : 2 * p + 2].reshape(64, 64), top_ref[p])
+        mom2[p] = (both[0:32, 0:64] + both[32:64, 64:128]).astype(BF16)
     for a, core, j in received:
         both = got_ref[core, j, 0:32, :]
         mom0[2 * a] = both[:, 0:64]
         mom0[2 * a + 1] = both[:, 64:128]
     for p in range(8):
-        mom3[p] = (dot(mom2[2 * p], matrix(top_ref, 32 + 2 * p)) + dot(mom2[2 * p + 1], matrix(top_ref, 33 + 2 * p))).astype(BF16)
-    for depth in range(4):
-        acc[depth][...] = jnp.zeros_like(acc[depth])
-    for s in range(32):
-        for depth in (0, 1):
-            first, second = cols_ref[depth, s], cols_ref[depth + 2, s]
-            picked = jnp.concatenate([mom[depth][first], mom[depth + 2][second]], axis=0)
-            term = dot(picked, coupling_ref[depth * 32 + s])
-            acc[depth][rows_ref[depth, s]] += term[0:32, 0:64]
-            acc[depth + 2][rows_ref[depth + 2, s], :, 64:128] += term[32:64, 64:128]
+        both = dot(mom2[2 * p : 2 * p + 2].reshape(64, 64), top_ref[16 + p])
+        mom3[p] = (both[0:32, 0:64] + both[32:64, 64:128]).astype(BF16)
+    for depth in (0, 2):
+        for s in range(32):
+            first, second = cols_ref[depth, s], cols_ref[depth + 1, s]
+            picked = jnp.concatenate([mom[depth][first], mom[depth + 1][second]], axis=0)
+            term = dot(picked, coupling_ref[depth * 16 + s])
+            acc[depth][rows_ref[depth, s], :, 0:64] += term[0:32, 0:64]
+            acc[depth + 1][rows_ref[depth + 1, s], :, 64:128] += term[32:64, 64:128]
+    tops = [acc3[p].astype(BF16) for p in range(4)]
     for j, b in enumerate(COL_ORDER):
-        upper = jnp.concatenate([acc1[b], acc2[b // 2, :, 64:128], acc3[b // 4, :, 64:128]], axis=1).astype(BF16)
+        upper = jnp.concatenate([(acc1[b] + acc2[b // 2]).astype(BF16), tops[b // 4]], axis=1)
         own = jnp.concatenate([acc0[2 * b], acc0[2 * b + 1]], axis=1)
         out_ref[j] = (own + dot(upper, down_ref[b])).astype(BF16)
 
@@ -146,6 +142,48 @@
     for i in range(2):
         distant = dot(leaf_local[:, 64 * i : 64 * (i + 1)], basis_ref[i])
         out_ref[:, 256 * i : 256 * (i + 1)] = (distant + near_ref[i]).astype(BF16)
+
+
+def call_prepare(*operands):
+    return pl.pallas_call(
+        prepare_kernel,
+        out_shape=[
+            pltpu.VMEM((64, 64, 128), BF16),
+            pltpu.VMEM((24, 64, 128), BF16),
+            pltpu.VMEM((16, 256, 128), BF16),
+            pltpu.SMEM((4, 32), jnp.int32),
+            pltpu.SMEM((4, 32), jnp.int32),
+            pltpu.VMEM((2, 32, 256), F32),
+        ],
+        in_specs=[pl.BlockSpec(memory_space=pl.ANY)] * 9,
+        out_specs=[vmem()] * 3 + [smem()] * 2 + [vmem()],
+        scratch_shapes=[
+            pltpu.VMEM((128, 4096), BF16),
+            pltpu.VMEM((48, 4096), BF16),
+            pltpu.VMEM((56, 4096), BF16),
+            pltpu.VMEM((8, 256, 256), BF16),
+            pltpu.VMEM((32, 512), BF16),
+            pltpu.SMEM((8,), jnp.int32),
+            pltpu.SMEM((8,), jnp.int32),
+            pltpu.SemaphoreType.DMA((9,)),
+        ],
+        compiler_params=pltpu.CompilerParams(vmem_limit_bytes=60 * 1024 * 1024),
+        cost_estimate=pl.CostEstimate(flops=33_554_432, bytes_accessed=8_000_000, transcendentals=0),
+        name="prepare",
+    )(*operands)
+
+
+def call_trees(*operands):
+    return pl.pallas_call(
+        tree_kernel,
+        out_shape=jax.ShapeDtypeStruct((16, 32, 128), BF16),
+        in_specs=[smem()] * 2 + [vmem()] * 4,
+        out_specs=vmem(),
+        scratch_shapes=[pltpu.VMEM((64 >> depth, 32, 64), BF16) for depth in range(4)]
+        + [pltpu.VMEM((32 >> depth, 32, 128 if depth else 64), F32) for depth in range(4)],
+        compiler_params=pltpu.CompilerParams(vmem_limit_bytes=16 * 1024 * 1024),
+        name="trees",
+    )(*operands)
 
 
 def local(
@@ -172,47 +210,13 @@
     same_core = [[2 * chip + core for chip in CHIP_ORDER] for core in range(2)]
     same_chip = [[2 * chip, 2 * chip + 1] for chip in range(16)]
     arrived = lax.all_to_all(message, "row", 0, 0, axis_index_groups=same_core)
-    blocks, up, down, rows, cols, nearby = pl.pallas_call(
-        prepare_kernel,
-        out_shape=[
-            pltpu.VMEM((64, 64, 128), BF16),
-            pltpu.VMEM((24, 64, 128), BF16),
-            pltpu.VMEM((16, 192, 128), BF16),
-            pltpu.SMEM((4, 32), jnp.int32),
-            pltpu.SMEM((4, 32), jnp.int32),
-            pltpu.VMEM((2, 32, 256), F32),
-        ],
-        in_specs=[pl.BlockSpec(memory_space=pl.ANY)] * 9,
-        out_specs=[vmem()] * 3 + [smem()] * 2 + [vmem()],
-        scratch_shapes=[
-            pltpu.VMEM((128, 4096), BF16),
-            pltpu.VMEM((48, 4096), BF16),
-            pltpu.VMEM((56, 4096), BF16),
-            pltpu.VMEM((8, 256, 256), BF16),
-            pltpu.VMEM((32, 512), BF16),
-            pltpu.SMEM((8,), jnp.int32),
-            pltpu.SMEM((8,), jnp.int32),
-            pltpu.SemaphoreType.DMA((9,)),
-        ],
-        compiler_params=pltpu.CompilerParams(vmem_limit_bytes=60 * 1024 * 1024),
-        cost_estimate=pl.CostEstimate(flops=33_554_432, bytes_accessed=8_000_000, transcendentals=0),
-        name="prepare",
-    )(
+    blocks, up, down, rows, cols, nearby = call_prepare(
         coupling, col_top_links, row_links, coupling_rows, coupling_cols,
         near_blocks, columns_x, near_rows, near_cols,
     )
     arrived, nearby = lax.optimization_barrier((arrived, nearby))
     gathered = lax.all_gather(arrived, "row", axis=0, axis_index_groups=same_chip)
-    partials = pl.pallas_call(
-        tree_kernel,
-        out_shape=jax.ShapeDtypeStruct((16, 32, 128), BF16),
-        in_specs=[smem()] * 2 + [vmem()] * 4,
-        out_specs=vmem(),
-        scratch_shapes=[pltpu.VMEM((64 >> depth, 32, 64), BF16) for depth in range(4)]
-        + [pltpu.VMEM((32 >> depth, 32, 64 if depth < 2 else 128), F32) for depth in range(4)],
-        compiler_params=pltpu.CompilerParams(vmem_limit_bytes=16 * 1024 * 1024),
-        name="trees",
-    )(rows, cols, gathered, up, blocks, down)
+    partials = call_trees(rows, cols, gathered, up, blocks, down)
     scattered = lax.all_to_all(partials, "col", 0, 0, axis_index_groups=[COL_ORDER])
     return pl.pallas_call(
         output_kernel,

time: 44.9 us -> 44.1 us (0.982)
  blocking collectives: 28.1 us -> 27.3 us
    all_to_all x1, blocking collectives: 21.4 us -> 20.6 us  [local(): lax.all_to_all(partials, 'col', 0, 0, axis_index_groups=[COL_ORDER])]
  transfers between devices with their start and end apart: 1 -> 1, of which waited for: 0 -> 0; matrix products, arithmetic and copies ran while one was open for 0% -> 0% of each run, Pallas kernels for 6% -> 7%
where the time goes in v8:
time: 44.1 us; the launch traced here: 43.7 us
  blocking collectives  27.3 us (62%)
  starting transfers between devices  9.55 us (22%)
  Pallas kernels  6.81 us (15%)
    all_to_all x1, blocking collectives, local(): lax.all_to_all(partials, 'col', 0, 0, axis_index_groups=[COL_ORDER])  20.6 us
    all_to_all x1, starting transfers between devices, local(): arrived = lax.all_to_all(message, 'row', 0, 0, axis_index_groups=same_core)  9.55 us
    all_gather x1, blocking collectives, local(): lax.all_gather(arrived, 'row', axis=0, axis_index_groups=same_chip)  6.68 us
    pallas_call x1, Pallas kernels, call_prepare(): pl.pallas_call(prepare_kernel, out_shape=[pltpu.VMEM((64, 64, 128), BF16)...  2.91 us
    pallas_call x1, Pallas kernels, local(): pl.pallas_call(moments_kernel, out_shape=jax.ShapeDtypeStruct((16, 48, 12...  1.84 us
    pallas_call x1, Pallas kernels, call_trees(): pl.pallas_call(tree_kernel, out_shape=jax.ShapeDtypeStruct((16, 32, 128),...  1.23 us
  transfers between devices with their start and end apart: 1, of which 0 were waited for; matrix products, arithmetic and copies ran while one was open for 0% of the time, Pallas kernels for 7%

profile of v8, /device:TPU:1, one launch (start us, length us, event | category | flops | bytes accessed | tf_op | source)
XLA Modules:
  0.0 43.7 jit_solution(10884123889972524239)
XLA Ops:
  0.0 1.8 %moments.1 = bf16[16,48,128]{2,1,0:T(8,128)(2,1)} custom-call(bf16[32,512]{1,0:T(8,128)(2,1)} %x_ref.1, bf16[2,64,256]{2,1,0:T(8,128)(2,1)} %basis_ref.2, bf16[2,4096]{1,0:T(2,128)(2,1)} %links_ref.1), custom_call_target="tpu_custom_call" | custom-call | tf_op jit(solution)/shard_map/moments/pallas_call | solution.py:203
  1.8 9.5 %all-to-all-start = ((bf16[16,48,128]{2,1,0:T(8,128)(2,1)}), bf16[16,48,128]{2,1,0:T(8,128)(2,1)S(1)}, u32[]{:S(2)}, u32[]{:S(2)}) async-start(bf16[16,48,128]{2,1,0:T(8,128)(2,1)} %moments.1), calls=%async_computation | async-start | bytes 393216 | tf_op jit(solution)/shard_map/all_to_all | solution.py:212
  11.4 2.9 %prepare.1 = (bf16[64,64,128]{2,1,0:T(8,128)(2,1)S(1)}, bf16[24,64,128]{2,1,0:T(8,128)(2,1)S(1)}, bf16[16,256,128]{2,1,0:T(8,128)(2,1)S(1)}, s32[4,32]{1,0:T(4,1...) custom-call(bf16[128,4096]{1,0:T(8,128)(2,1)} %coupling_in.1, bf16[1,48,4096]{2,1,0:T(8,128)(2,1)} %top_in.1, ...), custom_call_target="tpu_custom_call" | custom-call | flops 33554432 | bytes 8000000 | tf_op jit(solution)/shard_map/prepare/pallas_call | solution.py:148
  14.3 0.0 all-to-all-done
  14.3 6.7 %all-gather = bf16[32,48,128]{2,1,0:T(8,128)(2,1)S(1)} all-gather(bf16[16,48,128]{2,1,0:T(8,128)(2,1)S(1)} %all-to-all-done), channel_id=2, replica_groups={{0,16},{32,48},{64,80},{96,112},{128,144},{160,176},{192,208},{224,240}..., dimensions={0}, use_global_device_ids=true | all-gather | bytes 589824 | tf_op jit(solution)/shard_map/all_gather | solution.py:218
  21.0 1.2 %trees.1 = bf16[16,32,128]{2,1,0:T(8,128)(2,1)S(1)} custom-call(s32[4,32]{1,0:T(4,128)S(4)} %get-tuple-element.13.rows_ref, s32[4,32]{1,0:T(4,128)S(4)} %get-tuple-element.14.cols_ref, bf16[2,16,48,128]{3,2,1,0:T(8,128)(2,1)S(1)} %bitcast.1, bf16[24,64,128]{2,1,0:T(8,128)(2,1)S(1)} %get-tuple-element.17.top_ref, ...), custom_call_target="tpu_custom_call" | custom-call | tf_op jit(solution)/shard_map/trees/pallas_call | solution.py:177
  22.2 0.0 copy-start
  22.3 20.6 %all_to_all.10.got_ref = bf16[16,32,128]{2,1,0:T(8,128)(2,1)S(1)} all-to-all(bf16[16,32,128]{2,1,0:T(8,128)(2,1)S(1)} %trees.1), channel_id=1, replica_groups={{11,12,13,14,15,0,1,2,3,4,5,6,7,8,9,10},{27,28,29,30,31,16,17,18,19,20,..., dimensions={0} | all-to-all | bytes 262144 | tf_op jit(solution)/shard_map/all_to_all | solution.py:220
  42.9 0.0 copy-done
  42.9 0.8 %outputs.1 = bf16[32,512]{1,0:T(8,128)(2,1)} custom-call(bf16[16,32,128]{2,1,0:T(8,128)(2,1)S(1)} %all_to_all.10.got_ref, bf16[2,64,256]{2,1,0:T(8,128)(2,1)S(1)} %copy-done, f32[2,32,256]{2,1,0:T(8,128)S(1)} %get-tuple-element.20.near_ref), custom_call_target="tpu_custom_call" | custom-call | tf_op jit(solution)/shard_map/outputs/pallas_call | solution.py:221
Async XLA Ops:
  1.8 12.5 %all-to-all-start = ((bf16[16,48,128]{2,1,0:T(8,128)(2,1)}), bf16[16,48,128]{2,1,0:T(8,128)(2,1)S(1)}, u32[]{:S(2)}, u32[]{:S(2)}) async-start(bf16[16,48,128]{2,1,0:T(8,128)(2,1)} %moments.1), calls=%async_computation | async-start | bytes 393216 | tf_op jit(solution)/shard_map/all_to_all | solution.py:212
  22.2 20.6 %copy-start = (bf16[2,64,256]{2,1,0:T(8,128)(2,1)S(1)}, bf16[2,64,256]{2,1,0:T(8,128)(2,1)}, u32[]{:S(2)}) copy-start(bf16[2,64,256]{2,1,0:T(8,128)(2,1)} %basis_ref.3) | copy-start | bytes 196612

commit v9 on v8

--- a/solution.py
+++ b/solution.py
@@ -6,10 +6,13 @@
 from jax.sharding import PartitionSpec as P
 
 CHIP_ORDER = [(10 + j) % 16 for j in range(16)]
-COL_ORDER = [(11 + j) % 16 for j in range(16)]
 
 F32 = jnp.float32
 BF16 = jnp.bfloat16
+
+
+def col_start(row):
+    return 11 - 3 * ((row % 2) ^ (row < 2))
 
 
 def dot(a, b):
@@ -128,10 +131,11 @@
             acc[depth][rows_ref[depth, s], :, 0:64] += term[0:32, 0:64]
             acc[depth + 1][rows_ref[depth + 1, s], :, 64:128] += term[32:64, 64:128]
     tops = [acc3[p].astype(BF16) for p in range(4)]
-    for j, b in enumerate(COL_ORDER):
+    start = col_start(lax.axis_index("row"))
+    for b in range(16):
         upper = jnp.concatenate([(acc1[b] + acc2[b // 2]).astype(BF16), tops[b // 4]], axis=1)
         own = jnp.concatenate([acc0[2 * b], acc0[2 * b + 1]], axis=1)
-        out_ref[j] = (own + dot(upper, down_ref[b])).astype(BF16)
+        out_ref[lax.rem(16 + b - start, 16)] = (own + dot(upper, down_ref[b])).astype(BF16)
 
 
 def output_kernel(got_ref, basis_ref, near_ref, out_ref):
@@ -217,7 +221,8 @@
     arrived, nearby = lax.optimization_barrier((arrived, nearby))
     gathered = lax.all_gather(arrived, "row", axis=0, axis_index_groups=same_chip)
     partials = call_trees(rows, cols, gathered, up, blocks, down)
-    scattered = lax.all_to_all(partials, "col", 0, 0, axis_index_groups=[COL_ORDER])
+    same_row = [[16 * row + (col_start(row) + j) % 16 for j in range(16)] for row in range(32)]
+    scattered = lax.all_to_all(partials, ("row", "col"), 0, 0, axis_index_groups=same_row)
     return pl.pallas_call(
         output_kernel,
         out_shape=jax.ShapeDtypeStruct((32, 512), BF16),

time: 44.1 us -> 44.3 us (level)
  no operation moved by 1% of the time
where the time goes in v9:
time: 44.3 us; the launch traced here: 44 us
  blocking collectives  27.7 us (63%)
  starting transfers between devices  9.55 us (22%)
  Pallas kernels  6.79 us (15%)
    all_to_all x1, blocking collectives, local(): lax.all_to_all(partials, ('row', 'col'), 0, 0, axis_index_groups=same_row)  21 us
    all_to_all x1, starting transfers between devices, local(): arrived = lax.all_to_all(message, 'row', 0, 0, axis_index_groups=same_core)  9.55 us
    all_gather x1, blocking collectives, local(): lax.all_gather(arrived, 'row', axis=0, axis_index_groups=same_chip)  6.68 us
    pallas_call x1, Pallas kernels, call_prepare(): pl.pallas_call(prepare_kernel, out_shape=[pltpu.VMEM((64, 64, 128), BF16)...  2.91 us
    pallas_call x1, Pallas kernels, local(): pl.pallas_call(moments_kernel, out_shape=jax.ShapeDtypeStruct((16, 48, 12...  1.84 us
    pallas_call x1, Pallas kernels, call_trees(): pl.pallas_call(tree_kernel, out_shape=jax.ShapeDtypeStruct((16, 32, 128),...  1.21 us
  transfers between devices with their start and end apart: 1, of which 0 were waited for; matrix products, arithmetic and copies ran while one was open for 0% of the time, Pallas kernels for 7%

profile of v9, /device:TPU:1, one launch (start us, length us, event | category | flops | bytes accessed | tf_op | source)
XLA Modules:
  0.0 44.0 jit_solution(10679155594911036892)
XLA Ops:
  0.0 1.8 %moments.1 = bf16[16,48,128]{2,1,0:T(8,128)(2,1)} custom-call(bf16[32,512]{1,0:T(8,128)(2,1)} %x_ref.1, bf16[2,64,256]{2,1,0:T(8,128)(2,1)} %basis_ref.2, bf16[2,4096]{1,0:T(2,128)(2,1)} %links_ref.1), custom_call_target="tpu_custom_call" | custom-call | tf_op jit(solution)/shard_map/moments/pallas_call | solution.py:207
  1.8 9.5 %all-to-all-start = ((bf16[16,48,128]{2,1,0:T(8,128)(2,1)}), bf16[16,48,128]{2,1,0:T(8,128)(2,1)S(1)}, u32[]{:S(2)}, u32[]{:S(2)}) async-start(bf16[16,48,128]{2,1,0:T(8,128)(2,1)} %moments.1), calls=%async_computation | async-start | bytes 393216 | tf_op jit(solution)/shard_map/all_to_all | solution.py:216
  11.4 2.9 %prepare.1 = (bf16[64,64,128]{2,1,0:T(8,128)(2,1)S(1)}, bf16[24,64,128]{2,1,0:T(8,128)(2,1)S(1)}, bf16[16,256,128]{2,1,0:T(8,128)(2,1)S(1)}, s32[4,32]{1,0:T(4,1...) custom-call(bf16[128,4096]{1,0:T(8,128)(2,1)} %coupling_in.1, bf16[1,48,4096]{2,1,0:T(8,128)(2,1)} %top_in.1, ...), custom_call_target="tpu_custom_call" | custom-call | flops 33554432 | bytes 8000000 | tf_op jit(solution)/shard_map/prepare/pallas_call | solution.py:152
  14.3 0.0 all-to-all-done
  14.3 6.7 %all-gather = bf16[32,48,128]{2,1,0:T(8,128)(2,1)S(1)} all-gather(bf16[16,48,128]{2,1,0:T(8,128)(2,1)S(1)} %all-to-all-done), channel_id=2, replica_groups={{0,16},{32,48},{64,80},{96,112},{128,144},{160,176},{192,208},{224,240}..., dimensions={0}, use_global_device_ids=true | all-gather | bytes 589824 | tf_op jit(solution)/shard_map/all_gather | solution.py:222
  21.0 1.2 %trees.1 = bf16[16,32,128]{2,1,0:T(8,128)(2,1)S(1)} custom-call(s32[4,32]{1,0:T(4,128)S(4)} %get-tuple-element.13.rows_ref, s32[4,32]{1,0:T(4,128)S(4)} %get-tuple-element.14.cols_ref, bf16[2,16,48,128]{3,2,1,0:T(8,128)(2,1)S(1)} %bitcast.1, bf16[24,64,128]{2,1,0:T(8,128)(2,1)S(1)} %get-tuple-element.17.top_ref, ...), custom_call_target="tpu_custom_call" | custom-call | tf_op jit(solution)/shard_map/trees/pallas_call | solution.py:181
  22.2 0.0 copy-start
  22.2 21.0 %all_to_all.10.got_ref = bf16[16,32,128]{2,1,0:T(8,128)(2,1)S(1)} all-to-all(bf16[16,32,128]{2,1,0:T(8,128)(2,1)S(1)} %trees.1), channel_id=1, replica_groups={{8,9,10,11,12,13,14,15,0,1,2,3,4,5,6,7},{27,28,29,30,31,16,17,18,19,20,..., dimensions={0} | all-to-all | bytes 262144 | tf_op jit(solution)/shard_map/all_to_all | solution.py:225
  43.2 0.0 copy-done
  43.2 0.8 %outputs.1 = bf16[32,512]{1,0:T(8,128)(2,1)} custom-call(bf16[16,32,128]{2,1,0:T(8,128)(2,1)S(1)} %all_to_all.10.got_ref, bf16[2,64,256]{2,1,0:T(8,128)(2,1)S(1)} %copy-done, f32[2,32,256]{2,1,0:T(8,128)S(1)} %get-tuple-element.20.near_ref), custom_call_target="tpu_custom_call" | custom-call | tf_op jit(solution)/shard_map/outputs/pallas_call | solution.py:226
Async XLA Ops:
  1.8 12.5 %all-to-all-start = ((bf16[16,48,128]{2,1,0:T(8,128)(2,1)}), bf16[16,48,128]{2,1,0:T(8,128)(2,1)S(1)}, u32[]{:S(2)}, u32[]{:S(2)}) async-start(bf16[16,48,128]{2,1,0:T(8,128)(2,1)} %moments.1), calls=%async_computation | async-start | bytes 393216 | tf_op jit(solution)/shard_map/all_to_all | solution.py:216
  22.2 21.0 %copy-start = (bf16[2,64,256]{2,1,0:T(8,128)(2,1)S(1)}, bf16[2,64,256]{2,1,0:T(8,128)(2,1)}, u32[]{:S(2)}) copy-start(bf16[2,64,256]{2,1,0:T(8,128)(2,1)} %basis_ref.3) | copy-start | bytes 196612

commit v10 on v9

--- a/solution.py
+++ b/solution.py
@@ -12,7 +12,7 @@
 
 
 def col_start(row):
-    return 11 - 3 * ((row % 2) ^ (row < 2))
+    return 11 - 3 * (row % 2)
 
 
 def dot(a, b):

time: 44.3 us -> 44 us (level); the launches traced: 44 us -> 43.2 us
  blocking collectives: 27.7 us -> 26.8 us
    all_to_all x1, blocking collectives: 21 us -> 20.1 us  [local(): lax.all_to_all(partials, ('row', 'col'), 0, 0, axis_index_groups=same_row)]
where the time goes in v10:
time: 44 us; the launch traced here: 43.2 us
  blocking collectives  26.8 us (61%)
  starting transfers between devices  9.55 us (22%)
  Pallas kernels  6.8 us (15%)
    all_to_all x1, blocking collectives, local(): lax.all_to_all(partials, ('row', 'col'), 0, 0, axis_index_groups=same_row)  20.1 us
    all_to_all x1, starting transfers between devices, local(): arrived = lax.all_to_all(message, 'row', 0, 0, axis_index_groups=same_core)  9.55 us
    all_gather x1, blocking collectives, local(): lax.all_gather(arrived, 'row', axis=0, axis_index_groups=same_chip)  6.68 us
    pallas_call x1, Pallas kernels, call_prepare(): pl.pallas_call(prepare_kernel, out_shape=[pltpu.VMEM((64, 64, 128), BF16)...  2.91 us
    pallas_call x1, Pallas kernels, local(): pl.pallas_call(moments_kernel, out_shape=jax.ShapeDtypeStruct((16, 48, 12...  1.84 us
    pallas_call x1, Pallas kernels, call_trees(): pl.pallas_call(tree_kernel, out_shape=jax.ShapeDtypeStruct((16, 32, 128),...  1.22 us
  transfers between devices with their start and end apart: 1, of which 0 were waited for; matrix products, arithmetic and copies ran while one was open for 0% of the time, Pallas kernels for 7%

profile of v10, /device:TPU:1, one launch (start us, length us, event | category | flops | bytes accessed | tf_op | source)
XLA Modules:
  0.0 43.2 jit_solution(8825807736233772466)
XLA Ops:
  0.0 1.8 %moments.1 = bf16[16,48,128]{2,1,0:T(8,128)(2,1)} custom-call(bf16[32,512]{1,0:T(8,128)(2,1)} %x_ref.1, bf16[2,64,256]{2,1,0:T(8,128)(2,1)} %basis_ref.2, bf16[2,4096]{1,0:T(2,128)(2,1)} %links_ref.1), custom_call_target="tpu_custom_call" | custom-call | tf_op jit(solution)/shard_map/moments/pallas_call | solution.py:207
  1.8 9.5 %all-to-all-start = ((bf16[16,48,128]{2,1,0:T(8,128)(2,1)}), bf16[16,48,128]{2,1,0:T(8,128)(2,1)S(1)}, u32[]{:S(2)}, u32[]{:S(2)}) async-start(bf16[16,48,128]{2,1,0:T(8,128)(2,1)} %moments.1), calls=%async_computation | async-start | bytes 393216 | tf_op jit(solution)/shard_map/all_to_all | solution.py:216
  11.4 2.9 %prepare.1 = (bf16[64,64,128]{2,1,0:T(8,128)(2,1)S(1)}, bf16[24,64,128]{2,1,0:T(8,128)(2,1)S(1)}, bf16[16,256,128]{2,1,0:T(8,128)(2,1)S(1)}, s32[4,32]{1,0:T(4,1...) custom-call(bf16[128,4096]{1,0:T(8,128)(2,1)} %coupling_in.1, bf16[1,48,4096]{2,1,0:T(8,128)(2,1)} %top_in.1, ...), custom_call_target="tpu_custom_call" | custom-call | flops 33554432 | bytes 8000000 | tf_op jit(solution)/shard_map/prepare/pallas_call | solution.py:152
  14.3 0.0 all-to-all-done
  14.3 6.7 %all-gather = bf16[32,48,128]{2,1,0:T(8,128)(2,1)S(1)} all-gather(bf16[16,48,128]{2,1,0:T(8,128)(2,1)S(1)} %all-to-all-done), channel_id=2, replica_groups={{0,16},{32,48},{64,80},{96,112},{128,144},{160,176},{192,208},{224,240}..., dimensions={0}, use_global_device_ids=true | all-gather | bytes 589824 | tf_op jit(solution)/shard_map/all_gather | solution.py:222
  21.0 1.2 %trees.1 = bf16[16,32,128]{2,1,0:T(8,128)(2,1)S(1)} custom-call(s32[4,32]{1,0:T(4,128)S(4)} %get-tuple-element.13.rows_ref, s32[4,32]{1,0:T(4,128)S(4)} %get-tuple-element.14.cols_ref, bf16[2,16,48,128]{3,2,1,0:T(8,128)(2,1)S(1)} %bitcast.1, bf16[24,64,128]{2,1,0:T(8,128)(2,1)S(1)} %get-tuple-element.17.top_ref, ...), custom_call_target="tpu_custom_call" | custom-call | tf_op jit(solution)/shard_map/trees/pallas_call | solution.py:181
  22.2 0.0 copy-start
  22.2 20.1 %all_to_all.10.got_ref = bf16[16,32,128]{2,1,0:T(8,128)(2,1)S(1)} all-to-all(bf16[16,32,128]{2,1,0:T(8,128)(2,1)S(1)} %trees.1), channel_id=1, replica_groups={{11,12,13,14,15,0,1,2,3,4,5,6,7,8,9,10},{24,25,26,27,28,29,30,31,16,17,..., dimensions={0} | all-to-all | bytes 262144 | tf_op jit(solution)/shard_map/all_to_all | solution.py:225
  42.4 0.0 copy-done
  42.4 0.8 %outputs.1 = bf16[32,512]{1,0:T(8,128)(2,1)} custom-call(bf16[16,32,128]{2,1,0:T(8,128)(2,1)S(1)} %all_to_all.10.got_ref, bf16[2,64,256]{2,1,0:T(8,128)(2,1)S(1)} %copy-done, f32[2,32,256]{2,1,0:T(8,128)S(1)} %get-tuple-element.20.near_ref), custom_call_target="tpu_custom_call" | custom-call | tf_op jit(solution)/shard_map/outputs/pallas_call | solution.py:226
Async XLA Ops:
  1.8 12.5 %all-to-all-start = ((bf16[16,48,128]{2,1,0:T(8,128)(2,1)}), bf16[16,48,128]{2,1,0:T(8,128)(2,1)S(1)}, u32[]{:S(2)}, u32[]{:S(2)}) async-start(bf16[16,48,128]{2,1,0:T(8,128)(2,1)} %moments.1), calls=%async_computation | async-start | bytes 393216 | tf_op jit(solution)/shard_map/all_to_all | solution.py:216
  22.2 20.1 %copy-start = (bf16[2,64,256]{2,1,0:T(8,128)(2,1)S(1)}, bf16[2,64,256]{2,1,0:T(8,128)(2,1)}, u32[]{:S(2)}) copy-start(bf16[2,64,256]{2,1,0:T(8,128)(2,1)} %basis_ref.3) | copy-start | bytes 196612

commit v11 on v10

--- a/solution.py
+++ b/solution.py
@@ -12,7 +12,7 @@
 
 
 def col_start(row):
-    return 11 - 3 * (row % 2)
+    return 10 - 2 * (row % 2)
 
 
 def dot(a, b):

time: 44 us -> 45.1 us (1.025); the launches traced: 43.2 us -> 44.8 us
  blocking collectives: 26.8 us -> 28.4 us
    all_to_all x1, blocking collectives: 20.1 us -> 21.8 us  [local(): lax.all_to_all(partials, ('row', 'col'), 0, 0, axis_index_groups=same_row)]
where the time goes in v11:
time: 45.1 us; the launch traced here: 44.8 us
  blocking collectives  28.4 us (63%)
  starting transfers between devices  9.55 us (21%)
  Pallas kernels  6.79 us (15%)
    all_to_all x1, blocking collectives, local(): lax.all_to_all(partials, ('row', 'col'), 0, 0, axis_index_groups=same_row)  21.8 us
    all_to_all x1, starting transfers between devices, local(): arrived = lax.all_to_all(message, 'row', 0, 0, axis_index_groups=same_core)  9.55 us
    all_gather x1, blocking collectives, local(): lax.all_gather(arrived, 'row', axis=0, axis_index_groups=same_chip)  6.68 us
    pallas_call x1, Pallas kernels, call_prepare(): pl.pallas_call(prepare_kernel, out_shape=[pltpu.VMEM((64, 64, 128), BF16)...  2.91 us
    pallas_call x1, Pallas kernels, local(): pl.pallas_call(moments_kernel, out_shape=jax.ShapeDtypeStruct((16, 48, 12...  1.84 us
    pallas_call x1, Pallas kernels, call_trees(): pl.pallas_call(tree_kernel, out_shape=jax.ShapeDtypeStruct((16, 32, 128),...  1.21 us
  transfers between devices with their start and end apart: 1, of which 0 were waited for; matrix products, arithmetic and copies ran while one was open for 0% of the time, Pallas kernels for 7%

profile of v11, /device:TPU:1, one launch (start us, length us, event | category | flops | bytes accessed | tf_op | source)
XLA Modules:
  0.0 44.8 jit_solution(8864256230873153858)
XLA Ops:
  0.0 1.8 %moments.1 = bf16[16,48,128]{2,1,0:T(8,128)(2,1)} custom-call(bf16[32,512]{1,0:T(8,128)(2,1)} %x_ref.1, bf16[2,64,256]{2,1,0:T(8,128)(2,1)} %basis_ref.2, bf16[2,4096]{1,0:T(2,128)(2,1)} %links_ref.1), custom_call_target="tpu_custom_call" | custom-call | tf_op jit(solution)/shard_map/moments/pallas_call | solution.py:207
  1.8 9.5 %all-to-all-start = ((bf16[16,48,128]{2,1,0:T(8,128)(2,1)}), bf16[16,48,128]{2,1,0:T(8,128)(2,1)S(1)}, u32[]{:S(2)}, u32[]{:S(2)}) async-start(bf16[16,48,128]{2,1,0:T(8,128)(2,1)} %moments.1), calls=%async_computation | async-start | bytes 393216 | tf_op jit(solution)/shard_map/all_to_all | solution.py:216
  11.4 2.9 %prepare.1 = (bf16[64,64,128]{2,1,0:T(8,128)(2,1)S(1)}, bf16[24,64,128]{2,1,0:T(8,128)(2,1)S(1)}, bf16[16,256,128]{2,1,0:T(8,128)(2,1)S(1)}, s32[4,32]{1,0:T(4,1...) custom-call(bf16[128,4096]{1,0:T(8,128)(2,1)} %coupling_in.1, bf16[1,48,4096]{2,1,0:T(8,128)(2,1)} %top_in.1, ...), custom_call_target="tpu_custom_call" | custom-call | flops 33554432 | bytes 8000000 | tf_op jit(solution)/shard_map/prepare/pallas_call | solution.py:152
  14.3 0.0 all-to-all-done
  14.3 6.7 %all-gather = bf16[32,48,128]{2,1,0:T(8,128)(2,1)S(1)} all-gather(bf16[16,48,128]{2,1,0:T(8,128)(2,1)S(1)} %all-to-all-done), channel_id=2, replica_groups={{0,16},{32,48},{64,80},{96,112},{128,144},{160,176},{192,208},{224,240}..., dimensions={0}, use_global_device_ids=true | all-gather | bytes 589824 | tf_op jit(solution)/shard_map/all_gather | solution.py:222
  21.0 1.2 %trees.1 = bf16[16,32,128]{2,1,0:T(8,128)(2,1)S(1)} custom-call(s32[4,32]{1,0:T(4,128)S(4)} %get-tuple-element.13.rows_ref, s32[4,32]{1,0:T(4,128)S(4)} %get-tuple-element.14.cols_ref, bf16[2,16,48,128]{3,2,1,0:T(8,128)(2,1)S(1)} %bitcast.1, bf16[24,64,128]{2,1,0:T(8,128)(2,1)S(1)} %get-tuple-element.17.top_ref, ...), custom_call_target="tpu_custom_call" | custom-call | tf_op jit(solution)/shard_map/trees/pallas_call | solution.py:181
  22.2 0.0 copy-start
  22.2 21.8 %all_to_all.10.got_ref = bf16[16,32,128]{2,1,0:T(8,128)(2,1)S(1)} all-to-all(bf16[16,32,128]{2,1,0:T(8,128)(2,1)S(1)} %trees.1), channel_id=1, replica_groups={{10,11,12,13,14,15,0,1,2,3,4,5,6,7,8,9},{24,25,26,27,28,29,30,31,16,17,..., dimensions={0} | all-to-all | bytes 262144 | tf_op jit(solution)/shard_map/all_to_all | solution.py:225
  44.0 0.0 copy-done
  44.0 0.8 %outputs.1 = bf16[32,512]{1,0:T(8,128)(2,1)} custom-call(bf16[16,32,128]{2,1,0:T(8,128)(2,1)S(1)} %all_to_all.10.got_ref, bf16[2,64,256]{2,1,0:T(8,128)(2,1)S(1)} %copy-done, f32[2,32,256]{2,1,0:T(8,128)S(1)} %get-tuple-element.20.near_ref), custom_call_target="tpu_custom_call" | custom-call | tf_op jit(solution)/shard_map/outputs/pallas_call | solution.py:226
Async XLA Ops:
  1.8 12.5 %all-to-all-start = ((bf16[16,48,128]{2,1,0:T(8,128)(2,1)}), bf16[16,48,128]{2,1,0:T(8,128)(2,1)S(1)}, u32[]{:S(2)}, u32[]{:S(2)}) async-start(bf16[16,48,128]{2,1,0:T(8,128)(2,1)} %moments.1), calls=%async_computation | async-start | bytes 393216 | tf_op jit(solution)/shard_map/all_to_all | solution.py:216
  22.2 21.8 %copy-start = (bf16[2,64,256]{2,1,0:T(8,128)(2,1)S(1)}, bf16[2,64,256]{2,1,0:T(8,128)(2,1)}, u32[]{:S(2)}) copy-start(bf16[2,64,256]{2,1,0:T(8,128)(2,1)} %basis_ref.3) | copy-start | bytes 196612

commit v12 on v11

--- a/solution.py
+++ b/solution.py
@@ -6,13 +6,13 @@
 from jax.sharding import PartitionSpec as P
 
 CHIP_ORDER = [(10 + j) % 16 for j in range(16)]
+COL_ORDERS = (
+    [11, 1, 0, 3, 2, 5, 4, 7, 6, 15, 14, 13, 12, 10, 9, 8],
+    [8, 0, 1, 2, 3, 4, 5, 6, 7, 15, 14, 13, 12, 11, 10, 9],
+)
 
 F32 = jnp.float32
 BF16 = jnp.bfloat16
-
-
-def col_start(row):
-    return 10 - 2 * (row % 2)
 
 
 def dot(a, b):
@@ -131,11 +131,12 @@
             acc[depth][rows_ref[depth, s], :, 0:64] += term[0:32, 0:64]
             acc[depth + 1][rows_ref[depth + 1, s], :, 64:128] += term[32:64, 64:128]
     tops = [acc3[p].astype(BF16) for p in range(4)]
-    start = col_start(lax.axis_index("row"))
+    core = lax.rem(lax.axis_index("row"), 2)
     for b in range(16):
         upper = jnp.concatenate([(acc1[b] + acc2[b // 2]).astype(BF16), tops[b // 4]], axis=1)
         own = jnp.concatenate([acc0[2 * b], acc0[2 * b + 1]], axis=1)
-        out_ref[lax.rem(16 + b - start, 16)] = (own + dot(upper, down_ref[b])).astype(BF16)
+        place = jnp.where(core == 0, COL_ORDERS[0].index(b), COL_ORDERS[1].index(b))
+        out_ref[place] = (own + dot(upper, down_ref[b])).astype(BF16)
 
 
 def output_kernel(got_ref, basis_ref, near_ref, out_ref):
@@ -221,7 +222,7 @@
     arrived, nearby = lax.optimization_barrier((arrived, nearby))
     gathered = lax.all_gather(arrived, "row", axis=0, axis_index_groups=same_chip)
     partials = call_trees(rows, cols, gathered, up, blocks, down)
-    same_row = [[16 * row + (col_start(row) + j) % 16 for j in range(16)] for row in range(32)]
+    same_row = [[16 * row + z for z in COL_ORDERS[row % 2]] for row in range(32)]
     scattered = lax.all_to_all(partials, ("row", "col"), 0, 0, axis_index_groups=same_row)
     return pl.pallas_call(
         output_kernel,

time: 45.1 us -> 44.2 us (0.980)
  blocking collectives: 28.4 us -> 27.4 us
    all_to_all x1, blocking collectives: 21.8 us -> 20.7 us  [local(): lax.all_to_all(partials, ('row', 'col'), 0, 0, axis_index_groups=same_row)]
where the time goes in v12:
time: 44.2 us; the launch traced here: 43.7 us
  blocking collectives  27.4 us (62%)
  starting transfers between devices  9.55 us (22%)
  Pallas kernels  6.79 us (15%)
    all_to_all x1, blocking collectives, local(): lax.all_to_all(partials, ('row', 'col'), 0, 0, axis_index_groups=same_row)  20.7 us
    all_to_all x1, starting transfers between devices, local(): arrived = lax.all_to_all(message, 'row', 0, 0, axis_index_groups=same_core)  9.55 us
    all_gather x1, blocking collectives, local(): lax.all_gather(arrived, 'row', axis=0, axis_index_groups=same_chip)  6.69 us
    pallas_call x1, Pallas kernels, call_prepare(): pl.pallas_call(prepare_kernel, out_shape=[pltpu.VMEM((64, 64, 128), BF16)...  2.91 us
    pallas_call x1, Pallas kernels, local(): pl.pallas_call(moments_kernel, out_shape=jax.ShapeDtypeStruct((16, 48, 12...  1.84 us
    pallas_call x1, Pallas kernels, call_trees(): pl.pallas_call(tree_kernel, out_shape=jax.ShapeDtypeStruct((16, 32, 128),...  1.22 us
  transfers between devices with their start and end apart: 1, of which 0 were waited for; matrix products, arithmetic and copies ran while one was open for 0% of the time, Pallas kernels for 7%

profile of v12, /device:TPU:1, one launch (start us, length us, event | category | flops | bytes accessed | tf_op | source)
XLA Modules:
  0.0 43.7 jit_solution(6535267298468715469)
XLA Ops:
  0.0 1.8 %moments.1 = bf16[16,48,128]{2,1,0:T(8,128)(2,1)} custom-call(bf16[32,512]{1,0:T(8,128)(2,1)} %x_ref.1, bf16[2,64,256]{2,1,0:T(8,128)(2,1)} %basis_ref.2, bf16[2,4096]{1,0:T(2,128)(2,1)} %links_ref.1), custom_call_target="tpu_custom_call" | custom-call | tf_op jit(solution)/shard_map/moments/pallas_call | solution.py:208
  1.8 9.5 %all-to-all-start = ((bf16[16,48,128]{2,1,0:T(8,128)(2,1)}), bf16[16,48,128]{2,1,0:T(8,128)(2,1)S(1)}, u32[]{:S(2)}, u32[]{:S(2)}) async-start(bf16[16,48,128]{2,1,0:T(8,128)(2,1)} %moments.1), calls=%async_computation | async-start | bytes 393216 | tf_op jit(solution)/shard_map/all_to_all | solution.py:217
  11.4 2.9 %prepare.1 = (bf16[64,64,128]{2,1,0:T(8,128)(2,1)S(1)}, bf16[24,64,128]{2,1,0:T(8,128)(2,1)S(1)}, bf16[16,256,128]{2,1,0:T(8,128)(2,1)S(1)}, s32[4,32]{1,0:T(4,1...) custom-call(bf16[128,4096]{1,0:T(8,128)(2,1)} %coupling_in.1, bf16[1,48,4096]{2,1,0:T(8,128)(2,1)} %top_in.1, ...), custom_call_target="tpu_custom_call" | custom-call | flops 33554432 | bytes 8000000 | tf_op jit(solution)/shard_map/prepare/pallas_call | solution.py:153
  14.3 0.0 all-to-all-done
  14.3 6.7 %all-gather = bf16[32,48,128]{2,1,0:T(8,128)(2,1)S(1)} all-gather(bf16[16,48,128]{2,1,0:T(8,128)(2,1)S(1)} %all-to-all-done), channel_id=2, replica_groups={{0,16},{32,48},{64,80},{96,112},{128,144},{160,176},{192,208},{224,240}..., dimensions={0}, use_global_device_ids=true | all-gather | bytes 589824 | tf_op jit(solution)/shard_map/all_gather | solution.py:223
  21.0 1.2 %trees.1 = bf16[16,32,128]{2,1,0:T(8,128)(2,1)S(1)} custom-call(s32[4,32]{1,0:T(4,128)S(4)} %get-tuple-element.13.rows_ref, s32[4,32]{1,0:T(4,128)S(4)} %get-tuple-element.14.cols_ref, bf16[2,16,48,128]{3,2,1,0:T(8,128)(2,1)S(1)} %bitcast.1, bf16[24,64,128]{2,1,0:T(8,128)(2,1)S(1)} %get-tuple-element.17.top_ref, ...), custom_call_target="tpu_custom_call" | custom-call | tf_op jit(solution)/shard_map/trees/pallas_call | solution.py:182
  22.2 0.0 copy-start
  22.2 20.7 %all_to_all.10.got_ref = bf16[16,32,128]{2,1,0:T(8,128)(2,1)S(1)} all-to-all(bf16[16,32,128]{2,1,0:T(8,128)(2,1)S(1)} %trees.1), channel_id=1, replica_groups={{11,1,0,3,2,5,4,7,6,15,14,13,12,10,9,8},{24,16,17,18,19,20,21,22,23,31,..., dimensions={0} | all-to-all | bytes 262144 | tf_op jit(solution)/shard_map/all_to_all | solution.py:226
  42.9 0.0 copy-done
  42.9 0.8 %outputs.1 = bf16[32,512]{1,0:T(8,128)(2,1)} custom-call(bf16[16,32,128]{2,1,0:T(8,128)(2,1)S(1)} %all_to_all.10.got_ref, bf16[2,64,256]{2,1,0:T(8,128)(2,1)S(1)} %copy-done, f32[2,32,256]{2,1,0:T(8,128)S(1)} %get-tuple-element.20.near_ref), custom_call_target="tpu_custom_call" | custom-call | tf_op jit(solution)/shard_map/outputs/pallas_call | solution.py:227
Async XLA Ops:
  1.8 12.5 %all-to-all-start = ((bf16[16,48,128]{2,1,0:T(8,128)(2,1)}), bf16[16,48,128]{2,1,0:T(8,128)(2,1)S(1)}, u32[]{:S(2)}, u32[]{:S(2)}) async-start(bf16[16,48,128]{2,1,0:T(8,128)(2,1)} %moments.1), calls=%async_computation | async-start | bytes 393216 | tf_op jit(solution)/shard_map/all_to_all | solution.py:217
  22.2 20.7 %copy-start = (bf16[2,64,256]{2,1,0:T(8,128)(2,1)S(1)}, bf16[2,64,256]{2,1,0:T(8,128)(2,1)}, u32[]{:S(2)}) copy-start(bf16[2,64,256]{2,1,0:T(8,128)(2,1)} %basis_ref.3) | copy-start | bytes 196612

commit v13 on v12

--- a/solution.py
+++ b/solution.py
@@ -5,11 +5,8 @@
 from jax.experimental.pallas import tpu as pltpu
 from jax.sharding import PartitionSpec as P
 
-CHIP_ORDER = [(10 + j) % 16 for j in range(16)]
-COL_ORDERS = (
-    [11, 1, 0, 3, 2, 5, 4, 7, 6, 15, 14, 13, 12, 10, 9, 8],
-    [8, 0, 1, 2, 3, 4, 5, 6, 7, 15, 14, 13, 12, 11, 10, 9],
-)
+CHIP_ORDERS = [(10 + j) % 16 for j in range(16)], [(10 - j) % 16 for j in range(16)]
+COL_ORDERS = [(11 + j) % 16 for j in range(16)], [(8 - j) % 16 for j in range(16)]
 
 F32 = jnp.float32
 BF16 = jnp.bfloat16
@@ -108,7 +105,7 @@
     mom, acc = (mom0, mom1, mom2, mom3), (acc0, acc1, acc2, acc3)
     for depth in range(4):
         acc[depth][...] = jnp.zeros_like(acc[depth])
-    received = [(2 * chip + core, core, j) for j, chip in enumerate(CHIP_ORDER) for core in range(2)]
+    received = [(2 * CHIP_ORDERS[core][j] + core, core, j) for j in range(16) for core in range(2)]
     for a, core, j in received:
         parent = got_ref[core, j, 32:48, :]
         mom1[a, 0:16] = parent[:, 0:64]
@@ -212,7 +209,7 @@
         out_specs=vmem(),
         name="moments",
     )(columns_x, col_basis, col_links)
-    same_core = [[2 * chip + core for chip in CHIP_ORDER] for core in range(2)]
+    same_core = [[2 * chip + core for chip in CHIP_ORDERS[core]] for core in range(2)]
     same_chip = [[2 * chip, 2 * chip + 1] for chip in range(16)]
     arrived = lax.all_to_all(message, "row", 0, 0, axis_index_groups=same_core)
     blocks, up, down, rows, cols, nearby = call_prepare(

time: 44.2 us -> 45 us (1.018)
  blocking collectives: 27.4 us -> 28.3 us
    all_to_all x1, blocking collectives: 20.7 us -> 21.6 us  [local(): lax.all_to_all(partials, ('row', 'col'), 0, 0, axis_index_groups=same_row)]
where the time goes in v13:
time: 45 us; the launch traced here: 44.7 us
  blocking collectives  28.3 us (63%)
  starting transfers between devices  9.57 us (21%)
  Pallas kernels  6.8 us (15%)
    all_to_all x1, blocking collectives, local(): lax.all_to_all(partials, ('row', 'col'), 0, 0, axis_index_groups=same_row)  21.6 us
    all_to_all x1, starting transfers between devices, local(): arrived = lax.all_to_all(message, 'row', 0, 0, axis_index_groups=same_core)  9.57 us
    all_gather x1, blocking collectives, local(): lax.all_gather(arrived, 'row', axis=0, axis_index_groups=same_chip)  6.66 us
    pallas_call x1, Pallas kernels, call_prepare(): pl.pallas_call(prepare_kernel, out_shape=[pltpu.VMEM((64, 64, 128), BF16)...  2.91 us
    pallas_call x1, Pallas kernels, local(): pl.pallas_call(moments_kernel, out_shape=jax.ShapeDtypeStruct((16, 48, 12...  1.84 us
    pallas_call x1, Pallas kernels, call_trees(): pl.pallas_call(tree_kernel, out_shape=jax.ShapeDtypeStruct((16, 32, 128),...  1.23 us
  transfers between devices with their start and end apart: 1, of which 0 were waited for; matrix products, arithmetic and copies ran while one was open for 0% of the time, Pallas kernels for 7%

profile of v13, /device:TPU:1, one launch (start us, length us, event | category | flops | bytes accessed | tf_op | source)
XLA Modules:
  0.0 44.7 jit_solution(16269175579925946169)
XLA Ops:
  0.0 1.8 %moments.1 = bf16[16,48,128]{2,1,0:T(8,128)(2,1)} custom-call(bf16[32,512]{1,0:T(8,128)(2,1)} %x_ref.1, bf16[2,64,256]{2,1,0:T(8,128)(2,1)} %basis_ref.2, bf16[2,4096]{1,0:T(2,128)(2,1)} %links_ref.1), custom_call_target="tpu_custom_call" | custom-call | tf_op jit(solution)/shard_map/moments/pallas_call | solution.py:205
  1.8 9.6 %all-to-all-start = ((bf16[16,48,128]{2,1,0:T(8,128)(2,1)}), bf16[16,48,128]{2,1,0:T(8,128)(2,1)S(1)}, u32[]{:S(2)}, u32[]{:S(2)}) async-start(bf16[16,48,128]{2,1,0:T(8,128)(2,1)} %moments.1), calls=%async_computation | async-start | bytes 393216 | tf_op jit(solution)/shard_map/all_to_all | solution.py:214
  11.4 2.9 %prepare.1 = (bf16[64,64,128]{2,1,0:T(8,128)(2,1)S(1)}, bf16[24,64,128]{2,1,0:T(8,128)(2,1)S(1)}, bf16[16,256,128]{2,1,0:T(8,128)(2,1)S(1)}, s32[4,32]{1,0:T(4,1...) custom-call(bf16[128,4096]{1,0:T(8,128)(2,1)} %coupling_in.1, bf16[1,48,4096]{2,1,0:T(8,128)(2,1)} %top_in.1, ...), custom_call_target="tpu_custom_call" | custom-call | flops 33554432 | bytes 8000000 | tf_op jit(solution)/shard_map/prepare/pallas_call | solution.py:150
  14.3 0.0 all-to-all-done
  14.3 6.7 %all-gather = bf16[32,48,128]{2,1,0:T(8,128)(2,1)S(1)} all-gather(bf16[16,48,128]{2,1,0:T(8,128)(2,1)S(1)} %all-to-all-done), channel_id=2, replica_groups={{0,16},{32,48},{64,80},{96,112},{128,144},{160,176},{192,208},{224,240}..., dimensions={0}, use_global_device_ids=true | all-gather | bytes 589824 | tf_op jit(solution)/shard_map/all_gather | solution.py:220
  21.0 1.2 %trees.1 = bf16[16,32,128]{2,1,0:T(8,128)(2,1)S(1)} custom-call(s32[4,32]{1,0:T(4,128)S(4)} %get-tuple-element.13.rows_ref, s32[4,32]{1,0:T(4,128)S(4)} %get-tuple-element.14.cols_ref, bf16[2,16,48,128]{3,2,1,0:T(8,128)(2,1)S(1)} %bitcast.1, bf16[24,64,128]{2,1,0:T(8,128)(2,1)S(1)} %get-tuple-element.17.top_ref, ...), custom_call_target="tpu_custom_call" | custom-call | tf_op jit(solution)/shard_map/trees/pallas_call | solution.py:179
  22.2 0.0 copy-start
  22.2 21.6 %all_to_all.10.got_ref = bf16[16,32,128]{2,1,0:T(8,128)(2,1)S(1)} all-to-all(bf16[16,32,128]{2,1,0:T(8,128)(2,1)S(1)} %trees.1), channel_id=1, replica_groups={{11,12,13,14,15,0,1,2,3,4,5,6,7,8,9,10},{24,23,22,21,20,19,18,17,16,31,..., dimensions={0} | all-to-all | bytes 262144 | tf_op jit(solution)/shard_map/all_to_all | solution.py:223
  43.9 0.0 copy-done
  43.9 0.8 %outputs.1 = bf16[32,512]{1,0:T(8,128)(2,1)} custom-call(bf16[16,32,128]{2,1,0:T(8,128)(2,1)S(1)} %all_to_all.10.got_ref, bf16[2,64,256]{2,1,0:T(8,128)(2,1)S(1)} %copy-done, f32[2,32,256]{2,1,0:T(8,128)S(1)} %get-tuple-element.20.near_ref), custom_call_target="tpu_custom_call" | custom-call | tf_op jit(solution)/shard_map/outputs/pallas_call | solution.py:224
Async XLA Ops:
  1.8 12.5 %all-to-all-start = ((bf16[16,48,128]{2,1,0:T(8,128)(2,1)}), bf16[16,48,128]{2,1,0:T(8,128)(2,1)S(1)}, u32[]{:S(2)}, u32[]{:S(2)}) async-start(bf16[16,48,128]{2,1,0:T(8,128)(2,1)} %moments.1), calls=%async_computation | async-start | bytes 393216 | tf_op jit(solution)/shard_map/all_to_all | solution.py:214
  22.2 21.6 %copy-start = (bf16[2,64,256]{2,1,0:T(8,128)(2,1)S(1)}, bf16[2,64,256]{2,1,0:T(8,128)(2,1)}, u32[]{:S(2)}) copy-start(bf16[2,64,256]{2,1,0:T(8,128)(2,1)} %basis_ref.3) | copy-start | bytes 196612

commit v14 on v11

--- a/solution.py
+++ b/solution.py
@@ -12,7 +12,7 @@
 
 
 def col_start(row):
-    return 10 - 2 * (row % 2)
+    return 12 - 4 * (row % 2)
 
 
 def dot(a, b):

time: 45.1 us -> 43.8 us (0.971)
  blocking collectives: 28.4 us -> 27.1 us
    all_to_all x1, blocking collectives: 21.8 us -> 20.4 us  [local(): lax.all_to_all(partials, ('row', 'col'), 0, 0, axis_index_groups=same_row)]
where the time goes in v14:
time: 43.8 us; the launch traced here: 43.5 us
  blocking collectives  27.1 us (62%)
  starting transfers between devices  9.55 us (22%)
  Pallas kernels  6.8 us (16%)
    all_to_all x1, blocking collectives, local(): lax.all_to_all(partials, ('row', 'col'), 0, 0, axis_index_groups=same_row)  20.4 us
    all_to_all x1, starting transfers between devices, local(): arrived = lax.all_to_all(message, 'row', 0, 0, axis_index_groups=same_core)  9.55 us
    all_gather x1, blocking collectives, local(): lax.all_gather(arrived, 'row', axis=0, axis_index_groups=same_chip)  6.69 us
    pallas_call x1, Pallas kernels, call_prepare(): pl.pallas_call(prepare_kernel, out_shape=[pltpu.VMEM((64, 64, 128), BF16)...  2.91 us
    pallas_call x1, Pallas kernels, local(): pl.pallas_call(moments_kernel, out_shape=jax.ShapeDtypeStruct((16, 48, 12...  1.84 us
    pallas_call x1, Pallas kernels, call_trees(): pl.pallas_call(tree_kernel, out_shape=jax.ShapeDtypeStruct((16, 32, 128),...  1.23 us
  transfers between devices with their start and end apart: 1, of which 0 were waited for; matrix products, arithmetic and copies ran while one was open for 0% of the time, Pallas kernels for 7%

profile of v14, /device:TPU:1, one launch (start us, length us, event | category | flops | bytes accessed | tf_op | source)
XLA Modules:
  0.0 43.5 jit_solution(106868620163483392)
XLA Ops:
  0.0 1.8 %moments.1 = bf16[16,48,128]{2,1,0:T(8,128)(2,1)} custom-call(bf16[32,512]{1,0:T(8,128)(2,1)} %x_ref.1, bf16[2,64,256]{2,1,0:T(8,128)(2,1)} %basis_ref.2, bf16[2,4096]{1,0:T(2,128)(2,1)} %links_ref.1), custom_call_target="tpu_custom_call" | custom-call | tf_op jit(solution)/shard_map/moments/pallas_call | solution.py:207
  1.8 9.5 %all-to-all-start = ((bf16[16,48,128]{2,1,0:T(8,128)(2,1)}), bf16[16,48,128]{2,1,0:T(8,128)(2,1)S(1)}, u32[]{:S(2)}, u32[]{:S(2)}) async-start(bf16[16,48,128]{2,1,0:T(8,128)(2,1)} %moments.1), calls=%async_computation | async-start | bytes 393216 | tf_op jit(solution)/shard_map/all_to_all | solution.py:216
  11.4 2.9 %prepare.1 = (bf16[64,64,128]{2,1,0:T(8,128)(2,1)S(1)}, bf16[24,64,128]{2,1,0:T(8,128)(2,1)S(1)}, bf16[16,256,128]{2,1,0:T(8,128)(2,1)S(1)}, s32[4,32]{1,0:T(4,1...) custom-call(bf16[128,4096]{1,0:T(8,128)(2,1)} %coupling_in.1, bf16[1,48,4096]{2,1,0:T(8,128)(2,1)} %top_in.1, ...), custom_call_target="tpu_custom_call" | custom-call | flops 33554432 | bytes 8000000 | tf_op jit(solution)/shard_map/prepare/pallas_call | solution.py:152
  14.3 0.0 all-to-all-done
  14.3 6.7 %all-gather = bf16[32,48,128]{2,1,0:T(8,128)(2,1)S(1)} all-gather(bf16[16,48,128]{2,1,0:T(8,128)(2,1)S(1)} %all-to-all-done), channel_id=2, replica_groups={{0,16},{32,48},{64,80},{96,112},{128,144},{160,176},{192,208},{224,240}..., dimensions={0}, use_global_device_ids=true | all-gather | bytes 589824 | tf_op jit(solution)/shard_map/all_gather | solution.py:222
  21.0 1.2 %trees.1 = bf16[16,32,128]{2,1,0:T(8,128)(2,1)S(1)} custom-call(s32[4,32]{1,0:T(4,128)S(4)} %get-tuple-element.13.rows_ref, s32[4,32]{1,0:T(4,128)S(4)} %get-tuple-element.14.cols_ref, bf16[2,16,48,128]{3,2,1,0:T(8,128)(2,1)S(1)} %bitcast.1, bf16[24,64,128]{2,1,0:T(8,128)(2,1)S(1)} %get-tuple-element.17.top_ref, ...), custom_call_target="tpu_custom_call" | custom-call | tf_op jit(solution)/shard_map/trees/pallas_call | solution.py:181
  22.2 0.0 copy-start
  22.2 20.4 %all_to_all.10.got_ref = bf16[16,32,128]{2,1,0:T(8,128)(2,1)S(1)} all-to-all(bf16[16,32,128]{2,1,0:T(8,128)(2,1)S(1)} %trees.1), channel_id=1, replica_groups={{12,13,14,15,0,1,2,3,4,5,6,7,8,9,10,11},{24,25,26,27,28,29,30,31,16,17,..., dimensions={0} | all-to-all | bytes 262144 | tf_op jit(solution)/shard_map/all_to_all | solution.py:225
  42.7 0.0 copy-done
  42.7 0.8 %outputs.1 = bf16[32,512]{1,0:T(8,128)(2,1)} custom-call(bf16[16,32,128]{2,1,0:T(8,128)(2,1)S(1)} %all_to_all.10.got_ref, bf16[2,64,256]{2,1,0:T(8,128)(2,1)S(1)} %copy-done, f32[2,32,256]{2,1,0:T(8,128)S(1)} %get-tuple-element.20.near_ref), custom_call_target="tpu_custom_call" | custom-call | tf_op jit(solution)/shard_map/outputs/pallas_call | solution.py:226
Async XLA Ops:
  1.8 12.5 %all-to-all-start = ((bf16[16,48,128]{2,1,0:T(8,128)(2,1)}), bf16[16,48,128]{2,1,0:T(8,128)(2,1)S(1)}, u32[]{:S(2)}, u32[]{:S(2)}) async-start(bf16[16,48,128]{2,1,0:T(8,128)(2,1)} %moments.1), calls=%async_computation | async-start | bytes 393216 | tf_op jit(solution)/shard_map/all_to_all | solution.py:216
  22.2 20.5 %copy-start = (bf16[2,64,256]{2,1,0:T(8,128)(2,1)S(1)}, bf16[2,64,256]{2,1,0:T(8,128)(2,1)}, u32[]{:S(2)}) copy-start(bf16[2,64,256]{2,1,0:T(8,128)(2,1)} %basis_ref.3) | copy-start | bytes 196612

commit v15 on v14

--- a/solution.py
+++ b/solution.py
@@ -12,7 +12,7 @@
 
 
 def col_start(row):
-    return 12 - 4 * (row % 2)
+    return 12 - 4 * (row % 2) - (row < 1)
 
 
 def dot(a, b):

time: 43.8 us -> 43.8 us (level)
  no operation moved by 1% of the time
where the time goes in v15:
time: 43.8 us; the launch traced here: 43.3 us
  blocking collectives  26.9 us (61%)
  starting transfers between devices  9.55 us (22%)
  Pallas kernels  6.8 us (16%)
    all_to_all x1, blocking collectives, local(): lax.all_to_all(partials, ('row', 'col'), 0, 0, axis_index_groups=same_row)  20.2 us
    all_to_all x1, starting transfers between devices, local(): arrived = lax.all_to_all(message, 'row', 0, 0, axis_index_groups=same_core)  9.55 us
    all_gather x1, blocking collectives, local(): lax.all_gather(arrived, 'row', axis=0, axis_index_groups=same_chip)  6.69 us
    pallas_call x1, Pallas kernels, call_prepare(): pl.pallas_call(prepare_kernel, out_shape=[pltpu.VMEM((64, 64, 128), BF16)...  2.91 us
    pallas_call x1, Pallas kernels, local(): pl.pallas_call(moments_kernel, out_shape=jax.ShapeDtypeStruct((16, 48, 12...  1.84 us
    pallas_call x1, Pallas kernels, call_trees(): pl.pallas_call(tree_kernel, out_shape=jax.ShapeDtypeStruct((16, 32, 128),...  1.23 us
  transfers between devices with their start and end apart: 1, of which 0 were waited for; matrix products, arithmetic and copies ran while one was open for 0% of the time, Pallas kernels for 7%

profile of v15, /device:TPU:1, one launch (start us, length us, event | category | flops | bytes accessed | tf_op | source)
XLA Modules:
  0.0 43.3 jit_solution(15287360325841852661)
XLA Ops:
  0.0 1.8 %moments.1 = bf16[16,48,128]{2,1,0:T(8,128)(2,1)} custom-call(bf16[32,512]{1,0:T(8,128)(2,1)} %x_ref.1, bf16[2,64,256]{2,1,0:T(8,128)(2,1)} %basis_ref.2, bf16[2,4096]{1,0:T(2,128)(2,1)} %links_ref.1), custom_call_target="tpu_custom_call" | custom-call | tf_op jit(solution)/shard_map/moments/pallas_call | solution.py:207
  1.8 9.5 %all-to-all-start = ((bf16[16,48,128]{2,1,0:T(8,128)(2,1)}), bf16[16,48,128]{2,1,0:T(8,128)(2,1)S(1)}, u32[]{:S(2)}, u32[]{:S(2)}) async-start(bf16[16,48,128]{2,1,0:T(8,128)(2,1)} %moments.1), calls=%async_computation | async-start | bytes 393216 | tf_op jit(solution)/shard_map/all_to_all | solution.py:216
  11.4 2.9 %prepare.1 = (bf16[64,64,128]{2,1,0:T(8,128)(2,1)S(1)}, bf16[24,64,128]{2,1,0:T(8,128)(2,1)S(1)}, bf16[16,256,128]{2,1,0:T(8,128)(2,1)S(1)}, s32[4,32]{1,0:T(4,1...) custom-call(bf16[128,4096]{1,0:T(8,128)(2,1)} %coupling_in.1, bf16[1,48,4096]{2,1,0:T(8,128)(2,1)} %top_in.1, ...), custom_call_target="tpu_custom_call" | custom-call | flops 33554432 | bytes 8000000 | tf_op jit(solution)/shard_map/prepare/pallas_call | solution.py:152
  14.3 0.0 all-to-all-done
  14.3 6.7 %all-gather = bf16[32,48,128]{2,1,0:T(8,128)(2,1)S(1)} all-gather(bf16[16,48,128]{2,1,0:T(8,128)(2,1)S(1)} %all-to-all-done), channel_id=2, replica_groups={{0,16},{32,48},{64,80},{96,112},{128,144},{160,176},{192,208},{224,240}..., dimensions={0}, use_global_device_ids=true | all-gather | bytes 589824 | tf_op jit(solution)/shard_map/all_gather | solution.py:222
  21.0 1.2 %trees.1 = bf16[16,32,128]{2,1,0:T(8,128)(2,1)S(1)} custom-call(s32[4,32]{1,0:T(4,128)S(4)} %get-tuple-element.13.rows_ref, s32[4,32]{1,0:T(4,128)S(4)} %get-tuple-element.14.cols_ref, bf16[2,16,48,128]{3,2,1,0:T(8,128)(2,1)S(1)} %bitcast.1, bf16[24,64,128]{2,1,0:T(8,128)(2,1)S(1)} %get-tuple-element.17.top_ref, ...), custom_call_target="tpu_custom_call" | custom-call | tf_op jit(solution)/shard_map/trees/pallas_call | solution.py:181
  22.2 0.0 copy-start
  22.2 20.2 %all_to_all.10.got_ref = bf16[16,32,128]{2,1,0:T(8,128)(2,1)S(1)} all-to-all(bf16[16,32,128]{2,1,0:T(8,128)(2,1)S(1)} %trees.1), channel_id=1, replica_groups={{11,12,13,14,15,0,1,2,3,4,5,6,7,8,9,10},{24,25,26,27,28,29,30,31,16,17,..., dimensions={0} | all-to-all | bytes 262144 | tf_op jit(solution)/shard_map/all_to_all | solution.py:225
  42.4 0.0 copy-done
  42.4 0.8 %outputs.1 = bf16[32,512]{1,0:T(8,128)(2,1)} custom-call(bf16[16,32,128]{2,1,0:T(8,128)(2,1)S(1)} %all_to_all.10.got_ref, bf16[2,64,256]{2,1,0:T(8,128)(2,1)S(1)} %copy-done, f32[2,32,256]{2,1,0:T(8,128)S(1)} %get-tuple-element.20.near_ref), custom_call_target="tpu_custom_call" | custom-call | tf_op jit(solution)/shard_map/outputs/pallas_call | solution.py:226
Async XLA Ops:
  1.8 12.5 %all-to-all-start = ((bf16[16,48,128]{2,1,0:T(8,128)(2,1)}), bf16[16,48,128]{2,1,0:T(8,128)(2,1)S(1)}, u32[]{:S(2)}, u32[]{:S(2)}) async-start(bf16[16,48,128]{2,1,0:T(8,128)(2,1)} %moments.1), calls=%async_computation | async-start | bytes 393216 | tf_op jit(solution)/shard_map/all_to_all | solution.py:216
  22.2 20.2 %copy-start = (bf16[2,64,256]{2,1,0:T(8,128)(2,1)S(1)}, bf16[2,64,256]{2,1,0:T(8,128)(2,1)}, u32[]{:S(2)}) copy-start(bf16[2,64,256]{2,1,0:T(8,128)(2,1)} %basis_ref.3) | copy-start | bytes 196612
